TPU v7x, 512 devices: a whole 4x4x16 slice. The times are simulated.
512 devices in a mesh: sensor: 4 (over z_lo), gx: 16 (over x, y), gy: 8 (over z_hi, core).
Axes of the slice: x: 4, y: 4, z: 16 (z_hi: 4, z_lo: 4; z = z_hi * 4 + z_lo), core: 2. Of those that a mesh axis runs over, the one named last changes fastest.
Arguments:
- adjoint_last: float32 [4, 64, 256, 1024], P('sensor', None, 'gx', 'gy'), may hold values from -6 to 6
- adjoint_prev: float32 [4, 64, 256, 1024], P('sensor', None, 'gx', 'gy'), may hold values from -6 to 6
- adjoint_source: float32 [4, 6], P('sensor'), may hold values from -8 to 8
- sensor_cell: int32 [4], P('sensor'), may hold values from 0 to 4194303
- sound_class: int32 [64, 256, 1024], P(None, 'gx', 'gy'), may hold values from 0 to 7
- depth_index: int32 [256, 1024], P('gx', 'gy'), may hold values from 16 to 64
Outputs:
- adjoint_field: float32 [4, 64, 256, 1024], P('sensor', None, 'gx', 'gy')
- surface: float32 [4, 256, 1024], P('sensor', 'gx', 'gy')
- hessian: float32 [16, 8, 4, 4], P('gx', 'gy', 'sensor')
Inputs may be any that keep to these rules, and one draw needn't show every extreme that they name: `sensor_cell`: each sensor lies in the upper quarter of the levels, always in water.
All inputs are finite; a program needn't handle non-finite values.
Results may differ from a plain program's by a relative error of at most 0.0003.
Values sent between devices are 32-bit elements; how exact they have to be, the bound alone decides.
No kernel may reach another device: no remote copies, remote signals or barrier semaphores. Data moves between devices by JAX's collectives and lax.ppermute only.
A program may use at most 64 MiB of HBM per device.

v0:
```python
import jax
import jax.numpy as jnp
from jax import lax
from jax.sharding import PartitionSpec as P

STEPS = 6


COURANT_SQUARED = (0.08, 0.11, 0.14, 0.17, 0.2, 0.23, 0.26, 0.3)
SURFACE_RATE = 0.3


def padded_2(cells, sides, width):
    for axis, dim in sides:
        count = lax.axis_size(axis)
        ends = count - 1
        head = lax.slice_in_dim(cells, 0, width, axis=dim)
        tail = lax.slice_in_dim(cells, cells.shape[dim] - width, cells.shape[dim], axis=dim)
        cells = jnp.concatenate(
            [
                lax.ppermute(tail, axis, [(i, (i + 1) % count) for i in range(ends)]),
                cells,
                lax.ppermute(head, axis, [((i + 1) % count, i) for i in range(ends)]),
            ],
            axis=dim,
        )
    return cells


def speeds(category_ids):
    result = jnp.zeros(category_ids.shape, jnp.float32)
    for category, amount in enumerate(COURANT_SQUARED):
        result = result + (category_ids == category).astype(jnp.float32) * amount
    return result


def advance(padded, before, coef, water, source):
    core = padded[..., 1:-1, 1:-1]
    field = core[..., 1:, :, :]
    top_level = core[..., 0, :, :]
    above = core[..., :-1, :, :]
    below = jnp.concatenate([field[..., 1:, :, :], jnp.zeros_like(field[..., :1, :, :])], axis=-3)
    sides = padded[..., 1:, 2:, 1:-1] + padded[..., 1:, :-2, 1:-1]
    sides = sides + padded[..., 1:, 1:-1, 2:] + padded[..., 1:, 1:-1, :-2]
    laplace = sides + above + below - 6.0 * field
    fresh = water * (2.0 * field - before + coef * laplace + source)
    top_new = top_level + SURFACE_RATE * (fresh[..., 0, :, :] - top_level)
    return (fresh, top_new)


def source_hits(sensor_cell, levels, wide_x, wide_y, grid_x, grid_y, margin):
    start_x = lax.axis_index("gx") * (wide_x - 2 * margin) - margin
    start_y = lax.axis_index("gy") * (wide_y - 2 * margin) - margin
    level_ids = lax.broadcasted_iota(jnp.int32, (levels, wide_x, wide_y), 0)
    row_ids = lax.broadcasted_iota(jnp.int32, (levels, wide_x, wide_y), 1) + start_x
    col_ids = lax.broadcasted_iota(jnp.int32, (levels, wide_x, wide_y), 2) + start_y
    global_ids = level_ids * (grid_x * grid_y) + row_ids * grid_y + col_ids
    return (global_ids[None] == sensor_cell[:, None, None, None]).astype(jnp.float32)


def fold_trace(gram, pending, trace):
    return (gram, pending + [trace])


def on_device(adjoint_last, adjoint_prev, adjoint_source, sensor_cell, sound_class, depth_index):
    sens_local, levels, tile_x, tile_y = adjoint_last.shape
    grid_x = tile_x * lax.axis_size("gx")
    grid_y = tile_y * lax.axis_size("gy")
    all_sensors = sens_local * lax.axis_size("sensor")
    level_ids = lax.broadcasted_iota(jnp.int32, (levels, tile_x, tile_y), 0)
    coef = speeds(sound_class)
    water = (level_ids < depth_index[None]).astype(jnp.float32)
    seabed = (level_ids == depth_index[None] - 1).astype(jnp.float32)
    zeros_top = jnp.zeros((sens_local, 1, tile_x, tile_y), jnp.float32)
    state = jnp.concatenate([zeros_top, adjoint_last], 1)
    before = adjoint_prev
    gram = jnp.zeros((sens_local, all_sensors), jnp.float32)
    pending = []
    hits = source_hits(sensor_cell, levels, tile_x, tile_y, grid_x, grid_y, 0)
    for instant in range(STEPS):
        padded = padded_2(state, (("gx", 2), ("gy", 3)), 1)
        amounts = adjoint_source[:, instant][:, None, None, None]
        fresh, top_new = advance(padded, before, coef, water, hits * amounts)
        gram, pending = fold_trace(gram, pending, jnp.sum(fresh * seabed[None], axis=1))
        before = state[:, 1:]
        state = jnp.concatenate([top_new[:, None], fresh], 1)
    flat = jnp.stack(pending, 1).reshape(sens_local, -1)
    gram = jnp.einsum(
        "sf,kf->sk",
        flat,
        lax.all_gather(flat, "sensor", axis=0, tiled=True),
        precision=lax.Precision.HIGHEST,
        preferred_element_type=jnp.float32,
    )
    hessian = gram / (STEPS * tile_x * tile_y)
    return (state[:, 1:], state[:, 0], hessian[None, None])


def solution(mesh):
    return jax.shard_map(
        on_device,
        mesh=mesh,
        in_specs=(
            P("sensor", None, "gx", "gy"),
            P("sensor", None, "gx", "gy"),
            P("sensor", None),
            P("sensor"),
            P(None, "gx", "gy"),
            P("gx", "gy"),
        ),
        out_specs=(
            P("sensor", None, "gx", "gy"),
            P("sensor", "gx", "gy"),
            P("gx", "gy", "sensor", None),
        ),
        check_vma=False,
    )
```

profile of v0, /device:TPU:486, one launch (start us, length us, event | category | flops | bytes accessed | tf_op | source)
XLA Modules:
  0.0 199.4 jit_solution(928719890998171137)
XLA Ops:
  1.8 5.2 %collective-permute-start = (f32[1,65,1,128]{3,2,1,0:T(1,128)S(1)}, f32[1,65,1,128]{3,2,1,0:T(1,128)S(1)}, u32[]{:S(2)}, u32[]{:S(2)}) collective-permute-start(f32[1,65,1,128]{3,2,1,0:T(1,128)S(1)} %get-tuple-element.36), channel_id=1, source_target_pairs={{8,0},{16,8},{24,16},{32,24},{40,32},{48,40},{56,48},{64,56},{72,6... | collective-permute-start | bytes 99848 | tf_op jit(solution)/shard_map/ppermute | solution.py:23
  10.3 4.6 %collective-permute-done.1 = f32[1,65,1,128]{3,2,1,0:T(1,128)S(1)} collective-permute-done((f32[1,65,1,128]{3,2,1,0:T(1,128)S(1)}, f32[1,65,1,128]{3,2,1,0:T(1,128)S(1)}, u32[]{:S(2)}, u32[]{:S(2)}) %collective-permute-start.1) | collective-permute-done | bytes 33312 | tf_op jit(solution)/shard_map/ppermute | solution.py:21
  17.6 3.5 %collective-permute-start.2 = (f32[1,65,18,1]{1,3,2,0:T(1,128)S(1)}, f32[1,65,18,1]{1,3,2,0:T(1,128)S(1)}, u32[]{:S(2)}, u32[]{:S(2)}) collective-permute-start(f32[1,65,18,1]{1,3,2,0:T(1,128)S(1)} %copy.61), channel_id=1, source_target_pairs={{1,0},{2,1},{3,2},{4,3},{5,4},{6,5},{7,6},{9,8},{10,9},{11,10},{12... | collective-permute-start | bytes 14048 | tf_op jit(solution)/shard_map/ppermute | solution.py:23
  25.3 5.0 %collective-permute-done.3 = f32[1,65,18,1]{1,3,2,0:T(1,128)S(1)} collective-permute-done((f32[1,65,18,1]{1,3,2,0:T(1,128)S(1)}, f32[1,65,18,1]{1,3,2,0:T(1,128)S(1)}, u32[]{:S(2)}, u32[]{:S(2)}) %collective-permute-start.3) | collective-permute-done | bytes 4712 | tf_op jit(solution)/shard_map/ppermute | solution.py:21
  31.5 3.4 %fusion.59 = f32[1,64,16,128]{3,2,1,0:T(8,128)S(1)} fusion(f32[1,65,18,1]{3,2,1,0:T(8,128)} %copy.64, f32[1,65,1,128]{3,2,1,0:T(1,128)S(1)} %collective-permute-done, f32[1,65,16,128]{3,2,1,0:T(8,128)S(1)} %concatenate.132, f32[1,65,1,128]{3,2,1,0:T(1,128)S(1)} %collective-permute-done.1, f32[1,65,18,1]{3,2,1,0:T(8,128)} %copy.62, ...), kind=kLoop, calls=%fused_computation.132 | loop fusion | flops 6422528 | bytes 3755672 | tf_op jit(solution)/shard_map/mul | solution.py:46
  37.3 3.5 %collective-permute-start.5 = (f32[1,65,1,128]{3,2,1,0:T(1,128)S(1)}, f32[1,65,1,128]{3,2,1,0:T(1,128)S(1)}, u32[]{:S(2)}, u32[]{:S(2)}) collective-permute-start(f32[1,65,1,128]{3,2,1,0:T(1,128)S(1)} %get-tuple-element.33), channel_id=1, source_target_pairs={{0,8},{8,16},{16,24},{24,32},{32,40},{40,48},{48,56},{56,64},{64,7... | collective-permute-start | bytes 99848 | tf_op jit(solution)/shard_map/ppermute | solution.py:21
  40.8 4.4 %collective-permute-done.5 = f32[1,65,1,128]{3,2,1,0:T(1,128)S(1)} collective-permute-done((f32[1,65,1,128]{3,2,1,0:T(1,128)S(1)}, f32[1,65,1,128]{3,2,1,0:T(1,128)S(1)}, u32[]{:S(2)}, u32[]{:S(2)}) %collective-permute-start.5) | collective-permute-done | bytes 33312 | tf_op jit(solution)/shard_map/ppermute | solution.py:21
  54.2 5.2 %collective-permute-done.7 = f32[1,65,18,1]{1,3,2,0:T(1,128)S(1)} collective-permute-done((f32[1,65,18,1]{1,3,2,0:T(1,128)S(1)}, f32[1,65,18,1]{1,3,2,0:T(1,128)S(1)}, u32[]{:S(2)}, u32[]{:S(2)}) %collective-permute-start.7) | collective-permute-done | bytes 4712 | tf_op jit(solution)/shard_map/ppermute | solution.py:21
  60.7 3.3 %fusion.48 = f32[1,64,16,128]{3,2,1,0:T(8,128)S(1)} fusion(f32[1,64,16,128]{3,2,1,0:T(8,128)S(1)} %copy-done.1, f32[1,1,16,128]{3,2,1,0:T(8,128)S(1)} %slice_multiply_fusion, f32[1,65,18,1]{3,2,1,0:T(8,128)} %copy.68, f32[1,65,1,128]{3,2,1,0:T(1,128)S(1)} %collective-permute-done.4, f32[1,65,1,128]{3,2,1,0:T(1,128)S(1)} %collective-permute-done.5, ...), kind=kLoop, calls=%fused_computation.108 | loop fusion | flops 7077888 | bytes 2706392 | tf_op jit(solution)/shard_map/mul | solution.py:46
  66.0 3.9 %collective-permute-start.9 = (f32[1,65,1,128]{3,2,1,0:T(1,128)S(1)}, f32[1,65,1,128]{3,2,1,0:T(1,128)S(1)}, u32[]{:S(2)}, u32[]{:S(2)}) collective-permute-start(f32[1,65,1,128]{3,2,1,0:T(1,128)S(1)} %get-tuple-element.31), channel_id=1, source_target_pairs={{0,8},{8,16},{16,24},{24,32},{32,40},{40,48},{48,56},{56,64},{64,7... | collective-permute-start | bytes 99848 | tf_op jit(solution)/shard_map/ppermute | solution.py:21
  69.9 4.0 %collective-permute-done.9 = f32[1,65,1,128]{3,2,1,0:T(1,128)S(1)} collective-permute-done((f32[1,65,1,128]{3,2,1,0:T(1,128)S(1)}, f32[1,65,1,128]{3,2,1,0:T(1,128)S(1)}, u32[]{:S(2)}, u32[]{:S(2)}) %collective-permute-start.9) | collective-permute-done | bytes 33312 | tf_op jit(solution)/shard_map/ppermute | solution.py:21
  82.9 5.2 %collective-permute-done.11 = f32[1,65,18,1]{1,3,2,0:T(1,128)S(1)} collective-permute-done((f32[1,65,18,1]{1,3,2,0:T(1,128)S(1)}, f32[1,65,18,1]{1,3,2,0:T(1,128)S(1)}, u32[]{:S(2)}, u32[]{:S(2)}) %collective-permute-start.11) | collective-permute-done | bytes 4712 | tf_op jit(solution)/shard_map/ppermute | solution.py:21
  94.6 3.9 %collective-permute-start.13 = (f32[1,65,1,128]{3,2,1,0:T(1,128)S(1)}, f32[1,65,1,128]{3,2,1,0:T(1,128)S(1)}, u32[]{:S(2)}, u32[]{:S(2)}) collective-permute-start(f32[1,65,1,128]{3,2,1,0:T(1,128)S(1)} %get-tuple-element.29), channel_id=1, source_target_pairs={{0,8},{8,16},{16,24},{24,32},{32,40},{40,48},{48,56},{56,64},{64,7... | collective-permute-start | bytes 99848 | tf_op jit(solution)/shard_map/ppermute | solution.py:21
  98.6 4.0 %collective-permute-done.13 = f32[1,65,1,128]{3,2,1,0:T(1,128)S(1)} collective-permute-done((f32[1,65,1,128]{3,2,1,0:T(1,128)S(1)}, f32[1,65,1,128]{3,2,1,0:T(1,128)S(1)}, u32[]{:S(2)}, u32[]{:S(2)}) %collective-permute-start.13) | collective-permute-done | bytes 33312 | tf_op jit(solution)/shard_map/ppermute | solution.py:21
  112.6 5.2 %collective-permute-done.15 = f32[1,65,18,1]{1,3,2,0:T(1,128)S(1)} collective-permute-done((f32[1,65,18,1]{1,3,2,0:T(1,128)S(1)}, f32[1,65,18,1]{1,3,2,0:T(1,128)S(1)}, u32[]{:S(2)}, u32[]{:S(2)}) %collective-permute-start.15) | collective-permute-done | bytes 4712 | tf_op jit(solution)/shard_map/ppermute | solution.py:21
  119.0 3.3 %fusion.28 = f32[1,64,16,128]{3,2,1,0:T(8,128)S(1)} fusion(f32[1,64,16,128]{3,2,1,0:T(8,128)S(1)} %copy-done.5, f32[1,1,16,128]{3,2,1,0:T(8,128)S(1)} %multiply_add_fusion.2, f32[1,65,18,1]{3,2,1,0:T(8,128)} %copy.76, f32[1,65,1,128]{3,2,1,0:T(1,128)S(1)} %collective-permute-done.12, f32[1,65,1,128]{3,2,1,0:T(1,128)S(1)} %collective-permute-done.13, ...), kind=kLoop, calls=%fused_computation.62 | loop fusion | flops 7077888 | bytes 2706392 | tf_op jit(solution)/shard_map/mul | solution.py:46
  124.4 3.9 %collective-permute-start.17 = (f32[1,65,1,128]{3,2,1,0:T(1,128)S(1)}, f32[1,65,1,128]{3,2,1,0:T(1,128)S(1)}, u32[]{:S(2)}, u32[]{:S(2)}) collective-permute-start(f32[1,65,1,128]{3,2,1,0:T(1,128)S(1)} %get-tuple-element.27), channel_id=1, source_target_pairs={{0,8},{8,16},{16,24},{24,32},{32,40},{40,48},{48,56},{56,64},{64,7... | collective-permute-start | bytes 99848 | tf_op jit(solution)/shard_map/ppermute | solution.py:21
  128.3 4.0 %collective-permute-done.17 = f32[1,65,1,128]{3,2,1,0:T(1,128)S(1)} collective-permute-done((f32[1,65,1,128]{3,2,1,0:T(1,128)S(1)}, f32[1,65,1,128]{3,2,1,0:T(1,128)S(1)}, u32[]{:S(2)}, u32[]{:S(2)}) %collective-permute-start.17) | collective-permute-done | bytes 33312 | tf_op jit(solution)/shard_map/ppermute | solution.py:21
  142.5 5.0 %collective-permute-done.19 = f32[1,65,18,1]{1,3,2,0:T(1,128)S(1)} collective-permute-done((f32[1,65,18,1]{1,3,2,0:T(1,128)S(1)}, f32[1,65,18,1]{1,3,2,0:T(1,128)S(1)}, u32[]{:S(2)}, u32[]{:S(2)}) %collective-permute-start.19) | collective-permute-done | bytes 4712 | tf_op jit(solution)/shard_map/ppermute | solution.py:21
  154.0 3.9 %collective-permute-start.21 = (f32[1,65,1,128]{3,2,1,0:T(1,128)S(1)}, f32[1,65,1,128]{3,2,1,0:T(1,128)S(1)}, u32[]{:S(2)}, u32[]{:S(2)}) collective-permute-start(f32[1,65,1,128]{3,2,1,0:T(1,128)S(1)} %get-tuple-element.25), channel_id=1, source_target_pairs={{0,8},{8,16},{16,24},{24,32},{32,40},{40,48},{48,56},{56,64},{64,7... | collective-permute-start | bytes 99848 | tf_op jit(solution)/shard_map/ppermute | solution.py:21
  157.9 4.0 %collective-permute-done.21 = f32[1,65,1,128]{3,2,1,0:T(1,128)S(1)} collective-permute-done((f32[1,65,1,128]{3,2,1,0:T(1,128)S(1)}, f32[1,65,1,128]{3,2,1,0:T(1,128)S(1)}, u32[]{:S(2)}, u32[]{:S(2)}) %collective-permute-start.21) | collective-permute-done | bytes 33312 | tf_op jit(solution)/shard_map/ppermute | solution.py:21
  171.9 5.2 %collective-permute-done.23 = f32[1,65,18,1]{1,3,2,0:T(1,128)S(1)} collective-permute-done((f32[1,65,18,1]{1,3,2,0:T(1,128)S(1)}, f32[1,65,18,1]{1,3,2,0:T(1,128)S(1)}, u32[]{:S(2)}, u32[]{:S(2)}) %collective-permute-start.23) | collective-permute-done | bytes 4712 | tf_op jit(solution)/shard_map/ppermute | solution.py:21
  178.4 5.2 %select_reduce_fusion = (f32[16,128]{1,0:T(8,128)S(1)}, f32[16,128]{1,0:T(8,128)S(1)}, f32[16,128]{1,0:T(8,128)S(1)}, f32[16,128]{1,0:T(8,128)S(1)}, f32[16,128]...) fusion(s32[16,128]{1,0:T(8,128)S(1)} %broadcast_add_fusion, f32[1,64,16,128]{3,2,1,0:T(8,128)} %copy-done.9, ...), kind=kLoop, calls=%fused_computation.142 | loop fusion | flops 8769536 | bytes 4336600 | tf_op jit(solution)/shard_map/reduce_sum | solution.py:84
  183.7 13.6 %all-gather = f32[4,1,12288]{2,1,0:T(1,128)S(1)} all-gather(f32[1,1,12288]{2,1,0:T(1,128)S(1)} %bitcast.91), channel_id=1, replica_groups=mesh['sensor'=4,'gx'=16,'gy'=8] {'sensor'}, dimensions={0}, use_global_device_ids=true | all-gather | bytes 245760 | tf_op jit(solution)/shard_map/all_gather | solution.py:91
  (140 shorter events, 85.2 us)
Async XLA Ops:
  1.8 8.5 %collective-permute-start = (f32[1,65,1,128]{3,2,1,0:T(1,128)S(1)}, f32[1,65,1,128]{3,2,1,0:T(1,128)S(1)}, u32[]{:S(2)}, u32[]{:S(2)}) collective-permute-start(f32[1,65,1,128]{3,2,1,0:T(1,128)S(1)} %get-tuple-element.36), channel_id=1, source_target_pairs={{8,0},{16,8},{24,16},{32,24},{40,32},{48,40},{56,48},{64,56},{72,6... | collective-permute-start | bytes 99848 | tf_op jit(solution)/shard_map/ppermute | solution.py:23
  7.0 7.9 %collective-permute-start.1 = (f32[1,65,1,128]{3,2,1,0:T(1,128)S(1)}, f32[1,65,1,128]{3,2,1,0:T(1,128)S(1)}, u32[]{:S(2)}, u32[]{:S(2)}) collective-permute-start(f32[1,65,1,128]{3,2,1,0:T(1,128)S(1)} %get-tuple-element.35), channel_id=1, source_target_pairs={{0,8},{8,16},{16,24},{24,32},{32,40},{40,48},{48,56},{56,64},{64,7... | collective-permute-start | bytes 99848 | tf_op jit(solution)/shard_map/ppermute | solution.py:21
  17.6 6.4 %collective-permute-start.2 = (f32[1,65,18,1]{1,3,2,0:T(1,128)S(1)}, f32[1,65,18,1]{1,3,2,0:T(1,128)S(1)}, u32[]{:S(2)}, u32[]{:S(2)}) collective-permute-start(f32[1,65,18,1]{1,3,2,0:T(1,128)S(1)} %copy.61), channel_id=1, source_target_pairs={{1,0},{2,1},{3,2},{4,3},{5,4},{6,5},{7,6},{9,8},{10,9},{11,10},{12... | collective-permute-start | bytes 14048 | tf_op jit(solution)/shard_map/ppermute | solution.py:23
  21.3 8.9 %collective-permute-start.3 = (f32[1,65,18,1]{1,3,2,0:T(1,128)S(1)}, f32[1,65,18,1]{1,3,2,0:T(1,128)S(1)}, u32[]{:S(2)}, u32[]{:S(2)}) collective-permute-start(f32[1,65,18,1]{1,3,2,0:T(1,128)S(1)} %copy.63), channel_id=1, source_target_pairs={{0,1},{1,2},{2,3},{3,4},{4,5},{5,6},{6,7},{8,9},{9,10},{10,11},{11... | collective-permute-start | bytes 14048 | tf_op jit(solution)/shard_map/ppermute | solution.py:21
  35.0 5.9 %collective-permute-start.4 = (f32[1,65,1,128]{3,2,1,0:T(1,128)S(1)}, f32[1,65,1,128]{3,2,1,0:T(1,128)S(1)}, u32[]{:S(2)}, u32[]{:S(2)}) collective-permute-start(f32[1,65,1,128]{3,2,1,0:T(1,128)S(1)} %get-tuple-element.34), channel_id=1, source_target_pairs={{8,0},{16,8},{24,16},{32,24},{40,32},{48,40},{56,48},{64,56},{72,6... | collective-permute-start | bytes 99848 | tf_op jit(solution)/shard_map/ppermute | solution.py:23
  37.3 7.9 %collective-permute-start.5 = (f32[1,65,1,128]{3,2,1,0:T(1,128)S(1)}, f32[1,65,1,128]{3,2,1,0:T(1,128)S(1)}, u32[]{:S(2)}, u32[]{:S(2)}) collective-permute-start(f32[1,65,1,128]{3,2,1,0:T(1,128)S(1)} %get-tuple-element.33), channel_id=1, source_target_pairs={{0,8},{8,16},{16,24},{24,32},{32,40},{40,48},{48,56},{56,64},{64,7... | collective-permute-start | bytes 99848 | tf_op jit(solution)/shard_map/ppermute | solution.py:21
  48.3 4.6 %collective-permute-start.6 = (f32[1,65,18,1]{1,3,2,0:T(1,128)S(1)}, f32[1,65,18,1]{1,3,2,0:T(1,128)S(1)}, u32[]{:S(2)}, u32[]{:S(2)}) collective-permute-start(f32[1,65,18,1]{1,3,2,0:T(1,128)S(1)} %copy.65), channel_id=1, source_target_pairs={{1,0},{2,1},{3,2},{4,3},{5,4},{6,5},{7,6},{9,8},{10,9},{11,10},{12... | collective-permute-start | bytes 14048 | tf_op jit(solution)/shard_map/ppermute | solution.py:23
  50.5 8.9 %collective-permute-start.7 = (f32[1,65,18,1]{1,3,2,0:T(1,128)S(1)}, f32[1,65,18,1]{1,3,2,0:T(1,128)S(1)}, u32[]{:S(2)}, u32[]{:S(2)}) collective-permute-start(f32[1,65,18,1]{1,3,2,0:T(1,128)S(1)} %copy.67), channel_id=1, source_target_pairs={{0,1},{1,2},{2,3},{3,4},{4,5},{5,6},{6,7},{8,9},{9,10},{10,11},{11... | collective-permute-start | bytes 14048 | tf_op jit(solution)/shard_map/ppermute | solution.py:21
  64.0 5.9 %collective-permute-start.8 = (f32[1,65,1,128]{3,2,1,0:T(1,128)S(1)}, f32[1,65,1,128]{3,2,1,0:T(1,128)S(1)}, u32[]{:S(2)}, u32[]{:S(2)}) collective-permute-start(f32[1,65,1,128]{3,2,1,0:T(1,128)S(1)} %get-tuple-element.32), channel_id=1, source_target_pairs={{8,0},{16,8},{24,16},{32,24},{40,32},{48,40},{56,48},{64,56},{72,6... | collective-permute-start | bytes 99848 | tf_op jit(solution)/shard_map/ppermute | solution.py:23
  66.0 7.9 %collective-permute-start.9 = (f32[1,65,1,128]{3,2,1,0:T(1,128)S(1)}, f32[1,65,1,128]{3,2,1,0:T(1,128)S(1)}, u32[]{:S(2)}, u32[]{:S(2)}) collective-permute-start(f32[1,65,1,128]{3,2,1,0:T(1,128)S(1)} %get-tuple-element.31), channel_id=1, source_target_pairs={{0,8},{8,16},{16,24},{24,32},{32,40},{40,48},{48,56},{56,64},{64,7... | collective-permute-start | bytes 99848 | tf_op jit(solution)/shard_map/ppermute | solution.py:21
  76.9 4.7 %collective-permute-start.10 = (f32[1,65,18,1]{1,3,2,0:T(1,128)S(1)}, f32[1,65,18,1]{1,3,2,0:T(1,128)S(1)}, u32[]{:S(2)}, u32[]{:S(2)}) collective-permute-start(f32[1,65,18,1]{1,3,2,0:T(1,128)S(1)} %copy.69), channel_id=1, source_target_pairs={{1,0},{2,1},{3,2},{4,3},{5,4},{6,5},{7,6},{9,8},{10,9},{11,10},{12... | collective-permute-start | bytes 14048 | tf_op jit(solution)/shard_map/ppermute | solution.py:23
  79.2 8.9 %collective-permute-start.11 = (f32[1,65,18,1]{1,3,2,0:T(1,128)S(1)}, f32[1,65,18,1]{1,3,2,0:T(1,128)S(1)}, u32[]{:S(2)}, u32[]{:S(2)}) collective-permute-start(f32[1,65,18,1]{1,3,2,0:T(1,128)S(1)} %copy.71), channel_id=1, source_target_pairs={{0,1},{1,2},{2,3},{3,4},{4,5},{5,6},{6,7},{8,9},{9,10},{10,11},{11... | collective-permute-start | bytes 14048 | tf_op jit(solution)/shard_map/ppermute | solution.py:21
  92.7 5.9 %collective-permute-start.12 = (f32[1,65,1,128]{3,2,1,0:T(1,128)S(1)}, f32[1,65,1,128]{3,2,1,0:T(1,128)S(1)}, u32[]{:S(2)}, u32[]{:S(2)}) collective-permute-start(f32[1,65,1,128]{3,2,1,0:T(1,128)S(1)} %get-tuple-element.30), channel_id=1, source_target_pairs={{8,0},{16,8},{24,16},{32,24},{40,32},{48,40},{56,48},{64,56},{72,6... | collective-permute-start | bytes 99848 | tf_op jit(solution)/shard_map/ppermute | solution.py:23
  94.6 7.9 %collective-permute-start.13 = (f32[1,65,1,128]{3,2,1,0:T(1,128)S(1)}, f32[1,65,1,128]{3,2,1,0:T(1,128)S(1)}, u32[]{:S(2)}, u32[]{:S(2)}) collective-permute-start(f32[1,65,1,128]{3,2,1,0:T(1,128)S(1)} %get-tuple-element.29), channel_id=1, source_target_pairs={{0,8},{8,16},{16,24},{24,32},{32,40},{40,48},{48,56},{56,64},{64,7... | collective-permute-start | bytes 99848 | tf_op jit(solution)/shard_map/ppermute | solution.py:21
  105.5 5.8 %collective-permute-start.14 = (f32[1,65,18,1]{1,3,2,0:T(1,128)S(1)}, f32[1,65,18,1]{1,3,2,0:T(1,128)S(1)}, u32[]{:S(2)}, u32[]{:S(2)}) collective-permute-start(f32[1,65,18,1]{1,3,2,0:T(1,128)S(1)} %copy.73), channel_id=1, source_target_pairs={{1,0},{2,1},{3,2},{4,3},{5,4},{6,5},{7,6},{9,8},{10,9},{11,10},{12... | collective-permute-start | bytes 14048 | tf_op jit(solution)/shard_map/ppermute | solution.py:23
  108.9 8.9 %collective-permute-start.15 = (f32[1,65,18,1]{1,3,2,0:T(1,128)S(1)}, f32[1,65,18,1]{1,3,2,0:T(1,128)S(1)}, u32[]{:S(2)}, u32[]{:S(2)}) collective-permute-start(f32[1,65,18,1]{1,3,2,0:T(1,128)S(1)} %copy.75), channel_id=1, source_target_pairs={{0,1},{1,2},{2,3},{3,4},{4,5},{5,6},{6,7},{8,9},{9,10},{10,11},{11... | collective-permute-start | bytes 14048 | tf_op jit(solution)/shard_map/ppermute | solution.py:21
  122.4 5.9 %collective-permute-start.16 = (f32[1,65,1,128]{3,2,1,0:T(1,128)S(1)}, f32[1,65,1,128]{3,2,1,0:T(1,128)S(1)}, u32[]{:S(2)}, u32[]{:S(2)}) collective-permute-start(f32[1,65,1,128]{3,2,1,0:T(1,128)S(1)} %get-tuple-element.28), channel_id=1, source_target_pairs={{8,0},{16,8},{24,16},{32,24},{40,32},{48,40},{56,48},{64,56},{72,6... | collective-permute-start | bytes 99848 | tf_op jit(solution)/shard_map/ppermute | solution.py:23
  124.4 7.9 %collective-permute-start.17 = (f32[1,65,1,128]{3,2,1,0:T(1,128)S(1)}, f32[1,65,1,128]{3,2,1,0:T(1,128)S(1)}, u32[]{:S(2)}, u32[]{:S(2)}) collective-permute-start(f32[1,65,1,128]{3,2,1,0:T(1,128)S(1)} %get-tuple-element.27), channel_id=1, source_target_pairs={{0,8},{8,16},{16,24},{24,32},{32,40},{40,48},{48,56},{56,64},{64,7... | collective-permute-start | bytes 99848 | tf_op jit(solution)/shard_map/ppermute | solution.py:21
  135.2 5.9 %collective-permute-start.18 = (f32[1,65,18,1]{1,3,2,0:T(1,128)S(1)}, f32[1,65,18,1]{1,3,2,0:T(1,128)S(1)}, u32[]{:S(2)}, u32[]{:S(2)}) collective-permute-start(f32[1,65,18,1]{1,3,2,0:T(1,128)S(1)} %copy.77), channel_id=1, source_target_pairs={{1,0},{2,1},{3,2},{4,3},{5,4},{6,5},{7,6},{9,8},{10,9},{11,10},{12... | collective-permute-start | bytes 14048 | tf_op jit(solution)/shard_map/ppermute | solution.py:23
  138.6 8.9 %collective-permute-start.19 = (f32[1,65,18,1]{1,3,2,0:T(1,128)S(1)}, f32[1,65,18,1]{1,3,2,0:T(1,128)S(1)}, u32[]{:S(2)}, u32[]{:S(2)}) collective-permute-start(f32[1,65,18,1]{1,3,2,0:T(1,128)S(1)} %copy.79), channel_id=1, source_target_pairs={{0,1},{1,2},{2,3},{3,4},{4,5},{5,6},{6,7},{8,9},{9,10},{10,11},{11... | collective-permute-start | bytes 14048 | tf_op jit(solution)/shard_map/ppermute | solution.py:21
  152.1 5.9 %collective-permute-start.20 = (f32[1,65,1,128]{3,2,1,0:T(1,128)S(1)}, f32[1,65,1,128]{3,2,1,0:T(1,128)S(1)}, u32[]{:S(2)}, u32[]{:S(2)}) collective-permute-start(f32[1,65,1,128]{3,2,1,0:T(1,128)S(1)} %get-tuple-element.26), channel_id=1, source_target_pairs={{8,0},{16,8},{24,16},{32,24},{40,32},{48,40},{56,48},{64,56},{72,6... | collective-permute-start | bytes 99848 | tf_op jit(solution)/shard_map/ppermute | solution.py:23
  154.0 7.9 %collective-permute-start.21 = (f32[1,65,1,128]{3,2,1,0:T(1,128)S(1)}, f32[1,65,1,128]{3,2,1,0:T(1,128)S(1)}, u32[]{:S(2)}, u32[]{:S(2)}) collective-permute-start(f32[1,65,1,128]{3,2,1,0:T(1,128)S(1)} %get-tuple-element.25), channel_id=1, source_target_pairs={{0,8},{8,16},{16,24},{24,32},{32,40},{40,48},{48,56},{56,64},{64,7... | collective-permute-start | bytes 99848 | tf_op jit(solution)/shard_map/ppermute | solution.py:21
  164.9 5.8 %collective-permute-start.22 = (f32[1,65,18,1]{1,3,2,0:T(1,128)S(1)}, f32[1,65,18,1]{1,3,2,0:T(1,128)S(1)}, u32[]{:S(2)}, u32[]{:S(2)}) collective-permute-start(f32[1,65,18,1]{1,3,2,0:T(1,128)S(1)} %copy.81), channel_id=1, source_target_pairs={{1,0},{2,1},{3,2},{4,3},{5,4},{6,5},{7,6},{9,8},{10,9},{11,10},{12... | collective-permute-start | bytes 14048 | tf_op jit(solution)/shard_map/ppermute | solution.py:23
  168.2 8.9 %collective-permute-start.23 = (f32[1,65,18,1]{1,3,2,0:T(1,128)S(1)}, f32[1,65,18,1]{1,3,2,0:T(1,128)S(1)}, u32[]{:S(2)}, u32[]{:S(2)}) collective-permute-start(f32[1,65,18,1]{1,3,2,0:T(1,128)S(1)} %copy.83), channel_id=1, source_target_pairs={{0,1},{1,2},{2,3},{3,4},{4,5},{5,6},{6,7},{8,9},{9,10},{10,11},{11... | collective-permute-start | bytes 14048 | tf_op jit(solution)/shard_map/ppermute | solution.py:21
  (24 other events, 220.5 us)
where the time goes:
time: 201 us; the launch traced here: 199 us
  starting transfers between devices  63.5 us (32%)
  waiting for transfers between devices  55.5 us (28%)
  local copies, waits for them, and re-layouts  40 us (20%)
  other arithmetic  23.3 us (12%)
  blocking collectives  13.6 us (7%)
    ppermute x12, waiting for transfers between devices, padded_2(): lax.ppermute(tail, axis, [(i, (i + 1) % count) for i in range(ends)])  55.5 us
    ppermute x12, starting transfers between devices, padded_2(): lax.ppermute(tail, axis, [(i, (i + 1) % count) for i in range(ends)])  35.2 us
    ppermute x12, starting transfers between devices, padded_2(): lax.ppermute(head, axis, [((i + 1) % count, i) for i in range(ends)])  28.3 us
    slice x12, local copies, waits for them, and re-layouts, padded_2(): head = lax.slice_in_dim(cells, 0, width, axis=dim)  16.8 us
    mul x5, other arithmetic, advance(): fresh = water * (2.0 * field - before + coef * laplace + source)  16.5 us
    all_gather x1, blocking collectives, on_device(): lax.all_gather(flat, 'sensor', axis=0, tiled=True)  13.6 us
    ppermute x6, local copies, waits for them, and re-layouts, padded_2(): lax.ppermute(head, axis, [((i + 1) % count, i) for i in range(ends)])  7.74 us
    ppermute x6, local copies, waits for them, and re-layouts, padded_2(): lax.ppermute(tail, axis, [(i, (i + 1) % count) for i in range(ends)])  7.7 us
  transfers between devices with their start and end apart: 24, of which 12 were waited for; matrix products, arithmetic and copies ran while one was open for 7% of the time, Pallas kernels for 0%

commit v1 on v0

v1 whole, which is shorter than its diff:
```python
import functools

import jax
import jax.numpy as jnp
from jax import lax
from jax.experimental import pallas as pl
from jax.experimental.pallas import tpu as pltpu
from jax.sharding import PartitionSpec as P

STEPS = 6
COURANT_SQUARED = (0.08, 0.11, 0.14, 0.17, 0.2, 0.23, 0.26, 0.3)
SURFACE_RATE = 0.3

NZ, TX, TY = 64, 16, 128
HALO = 4
ROWS = TX + 2 * HALO
TOP = 8
DEEP = NZ + 16
CHUNK = 16
STRIP = 11
ITEMS = (("p0", 1), ("p0", 2), ("old", 1), ("p1", 2), ("p1", 3), ("p2", 3), ("wc", 1), ("wc", 2), ("p2", 4), ("wc", 3))
VMEM = pl.BlockSpec(memory_space=pltpu.VMEM)
SMEM = pl.BlockSpec(memory_space=pltpu.SMEM)
F32 = jnp.float32


def lanes(rows):
    return lax.broadcasted_iota(jnp.int32, (rows, TY), 1)


def rolled(values, shift):
    shift = shift % TY
    return values if shift == 0 else pltpu.roll(values, shift, axis=1)


def swap_pairs(count, first):
    return [pair for i in range(first, count - 1, 2) for pair in ((i, i + 1), (i + 1, i))]


def pack_kernel(last, prev, kind, depth, p0, old, wc, near, far):
    even = lax.rem(lax.axis_index("gy"), 2) == 0
    lane = lanes(NZ)
    level = lax.broadcasted_iota(jnp.int32, (NZ, TY), 0)

    def half(h, carry):
        left = jnp.zeros((NZ, TY), F32)
        right = jnp.zeros((NZ, TY), F32)
        for j in range(8):
            x = h * 8 + j
            here = pl.ds(x, NZ, stride=TX)
            now, before, k = last[here, :], prev[here, :], kind[here, :]
            coef = jnp.full((NZ, TY), COURANT_SQUARED[0], F32)
            for category in range(1, 8):
                coef = jnp.where(k == category, COURANT_SQUARED[category], coef)
            coef = jnp.where(level < depth[pl.ds(x, 1), :], coef, 0.0)
            p0[x], old[x], wc[x] = now, before, coef
            base = 16 * j
            for values, start, width in ((now, base, 6), (before, base + 6, 5), (coef, base + 11, 5)):
                mine = (lane >= start) & (lane < start + width)
                left = jnp.where(mine, rolled(values, start), left)
                right = jnp.where(mine, rolled(values, start - (TY - width)), right)
        near[h] = jnp.where(even, right, left)
        far[h] = jnp.where(even, left, right)
        return carry

    lax.fori_loop(0, 2, half, 0)


def update_row(now, old, wc, out, row, old_row, wc_row, out_row, depth_row=None):
    lane = lanes(CHUNK)
    trace = jnp.zeros((CHUNK, TY), F32)
    for start in range(0, NZ, CHUNK):
        at = pl.ds(TOP + start, CHUNK)
        centre = [now[row, t, at, :] for t in (0, 1)]
        down = [pltpu.roll(c, 1, axis=1) for c in centre]
        up = [pltpu.roll(c, TY - 1, axis=1) for c in centre]
        for t in (0, 1):
            beside = jnp.where(lane == 0, down[1 - t], down[t]) + jnp.where(lane == TY - 1, up[1 - t], up[t])
            rows = now[row - 1, t, at, :] + now[row + 1, t, at, :]
            levels = now[row, t, pl.ds(TOP + start - 1, CHUNK), :] + now[row, t, pl.ds(TOP + start + 1, CHUNK), :]
            laplace = (rows + beside) + levels - 6.0 * centre[t]
            coef = wc(wc_row, t, pl.ds(start, CHUNK))
            fresh = 2.0 * centre[t] - old(old_row, t, start) + coef * laplace
            fresh = jnp.where(coef > 0.0, fresh, 0.0)
            out[out_row, t, at, :] = fresh
            if t == 0 and depth_row is not None:
                level = lax.broadcasted_iota(jnp.int32, (CHUNK, TY), 0) + start
                trace = trace + jnp.where(level == depth_row - 1, fresh, 0.0)
            if start == 0:
                eta = now[row, t, TOP - 1 : TOP, :]
                out[out_row, t, TOP - 1 : TOP, :] = eta + SURFACE_RATE * (fresh[0:1] - eta)
    return jnp.sum(trace, axis=0, keepdims=True)


def sensor_place(cell):
    number = cell[0]
    size_y = TY * lax.axis_size("gy")
    plane = TX * lax.axis_size("gx") * size_y
    z = lax.div(number, plane)
    x = lax.div(lax.rem(number, plane), size_y) - TX * lax.axis_index("gx")
    y = lax.rem(number, size_y) - TY * lax.axis_index("gy")
    tile = jnp.where((y >= 0) & (y < TY), 0, 1)
    lane = lax.rem(y + 2 * size_y, TY)
    return z, x, tile, lane, (y >= -5) & (y < TY + 5)


def inject(out, row, place, amount):
    z, _, tile, lane, _ = place
    hit = jnp.where(lanes(1) == lane, amount, 0.0)
    at = pl.ds(TOP + z, 1)
    out[row, tile, at, :] = out[row, tile, at, :] + hit
    top = pl.ds(TOP - 1, 1)
    out[row, tile, top, :] = out[row, tile, top, :] + jnp.where(z == 0, SURFACE_RATE, 0.0) * hit
    return hit


def edge_kernel(p0, old, wc, near, far, cell, source, strip_a, strip_b, aux_p, aux_o, aux_w, e0, e1, e2):
    even = lax.rem(lax.axis_index("gy"), 2) == 0
    lane = lanes(NZ)
    for ref in (e0, e1):
        for x in range(TX):
            for t in (0, 1):
                ref[x, t, 0:TOP, :] = jnp.zeros((TOP, TY), F32)
                ref[x, t, TOP + NZ :, :] = jnp.zeros((8, TY), F32)

    def half(h, carry):
        from_right = jnp.where(even, near[h], far[h])
        from_left = jnp.where(even, far[h], near[h])
        for j in range(8):
            x = h * 8 + j
            base = 16 * j
            for ref, start, width in ((aux_p, base, 6), (aux_o, base + 6, 5), (aux_w, base + 11, 5)):
                right = rolled(from_right, -start)
                left = rolled(from_left, TY - width - start)
                ref[x] = jnp.where(lane < width, right, jnp.where(lane >= TY - width, left, 0.0))
            e0[x, 0, TOP : TOP + NZ, :] = p0[x]
            e0[x, 1, TOP : TOP + NZ, :] = aux_p[x]
        return carry

    lax.fori_loop(0, 2, half, 0)

    def old_0(x, t, start):
        return (old, aux_o)[t][x, pl.ds(start, CHUNK), :]

    def old_1(x, t, start):
        return e0[x, t, pl.ds(TOP + start, CHUNK), :]

    def coef(x, t, at):
        return (wc, aux_w)[t][x, at, :]

    place = sensor_place(cell)
    x_s, here = place[1], place[4]

    def first(i, carry):
        x = jnp.where(i < 4, 1 + i, 7 + i)
        update_row(e0, old_0, coef, e1, x, x, x, x)
        return carry

    lax.fori_loop(0, 8, first, 0)
    inside = here & (((x_s >= 1) & (x_s <= 4)) | ((x_s >= 11) & (x_s <= 14)))
    inject(e1, jnp.clip(x_s, 0, TX - 1), place, jnp.where(inside, source[0, 0], 0.0))

    def second(i, carry):
        x = jnp.where(i < 2, 2 + i, 10 + i)
        update_row(e1, old_1, coef, e2, x, x, x, x)
        return carry

    lax.fori_loop(0, 4, second, 0)
    inside = here & (((x_s >= 2) & (x_s <= 3)) | ((x_s >= 12) & (x_s <= 13)))
    inject(e2, jnp.clip(x_s, 0, TX - 1), place, jnp.where(inside, source[0, 1], 0.0))

    body = slice(TOP, TOP + NZ)
    upper_a = lax.rem(lax.axis_index("gx"), 2) == 0
    for strip, upper in ((strip_a, upper_a), (strip_b, ~upper_a)):
        corner = jnp.zeros((NZ, TY), F32)
        for k, (name, d) in enumerate(ITEMS):
            x = jnp.where(upper, TX - d, d - 1)
            if name == "old":
                main, aux = old[x], aux_o[x]
            elif name == "wc":
                main, aux = wc[x], aux_w[x]
            else:
                ref = {"p0": e0, "p1": e1, "p2": e2}[name]
                main, aux = ref[x, 0, body, :], ref[x, 1, body, :]
            strip[k] = main
            if k < 8:
                corner = jnp.where((lane >= 16 * k) & (lane < 16 * k + 16), rolled(aux, 8 + 16 * k), corner)
        strip[STRIP - 1] = corner


def steps_kernel(p0, old, wc, aux_p, aux_o, aux_w, strip_a, strip_b, depth, cell, source,
                 field, surface, trace, levels, coefs, depths, traces):
    body = slice(TOP, TOP + NZ)
    lane = lanes(NZ)
    depths[...] = jnp.zeros((ROWS, TY), jnp.int32)
    depths[HALO : HALO + TX, :] = depth[...]

    def blank(row, carry):
        for k in range(3):
            for t in (0, 1):
                levels[k, row, t, 0:TOP, :] = jnp.zeros((TOP, TY), F32)
                levels[k, row, t, TOP + NZ :, :] = jnp.zeros((8, TY), F32)
        return carry

    lax.fori_loop(0, ROWS, blank, 0)

    def fill(x, carry):
        row = x + HALO
        levels[1, row, 0, body, :] = p0[x]
        levels[1, row, 1, body, :] = aux_p[x]
        levels[0, row, 0, body, :] = old[x]
        levels[0, row, 1, body, :] = aux_o[x]
        coefs[row, 0] = wc[x]
        coefs[row, 1] = aux_w[x]
        return carry

    lax.fori_loop(0, TX, fill, 0)

    upper_a = lax.rem(lax.axis_index("gx"), 2) == 0
    for strip, upper in ((strip_a, upper_a), (strip_b, ~upper_a)):
        corner = strip[STRIP - 1]
        for k, (name, d) in enumerate(ITEMS):
            row = jnp.where(upper, HALO + TX - 1 + d, HALO - d)
            main = strip[k]
            if k < 8:
                aux = jnp.where((lane < 8) | (lane >= TY - 8), rolled(corner, -(8 + 16 * k)), 0.0)
            else:
                aux = jnp.zeros((NZ, TY), F32)
            for t, values in ((0, main), (1, aux)):
                if name == "wc":
                    coefs[row, t] = values
                    continue
                slot = {"old": 0, "p0": 1, "p1": 2, "p2": 0}[name]
                levels[slot, row, t, body, :] = values
                if name == "p1":
                    levels[2, row, t, TOP - 1 : TOP, :] = SURFACE_RATE * values[0:1]
                if name == "p2" and d == 3:
                    eta = levels[2, row, t, TOP - 1 : TOP, :]
                    levels[0, row, t, TOP - 1 : TOP, :] = eta + SURFACE_RATE * (values[0:1] - eta)

    place = sensor_place(cell)
    z_s, x_s, tile, _, here = place

    def coef(row, t, at):
        return coefs[row, t, at, :]

    for n, reach in zip(range(1, STEPS + 1), (1, 2, 3, 2, 1, 0)):
        now, before, out = levels.at[n % 3], levels.at[(n - 1) % 3], levels.at[(n + 1) % 3]

        def old_at(row, t, start):
            return before[row, t, pl.ds(TOP + start, CHUNK), :]

        def one(row, carry):
            sums = update_row(now, old_at, coef, out, row, row, row, row, depths[pl.ds(row, 1), :])
            traces[n - 1, pl.ds(row, 1), :] = sums
            return carry

        lax.fori_loop(HALO - reach, HALO + TX + reach, one, 0)
        inside = here & (x_s >= -reach) & (x_s < TX + reach)
        row_s = jnp.clip(x_s + HALO, 0, ROWS - 1)
        hit = inject(out, row_s, place, jnp.where(inside, source[0, n - 1], 0.0))
        at = pl.ds(row_s, 1)
        seabed = (depths[at, :] - 1 == z_s) & (tile == 0)
        traces[n - 1, at, :] = traces[n - 1, at, :] + jnp.where(seabed, hit, 0.0)

    final = levels.at[(STEPS + 1) % 3]

    def give(x, carry):
        field[pl.ds(x, NZ, stride=TX), :] = final[x + HALO, 0, body, :]
        surface[pl.ds(x, 1), :] = final[x + HALO, 0, TOP - 1 : TOP, :]
        return carry

    lax.fori_loop(0, TX, give, 0)
    for n in range(STEPS):
        rows = traces[n, HALO : HALO + TX, :]
        for s in range(trace.shape[0]):
            trace[s, n * TX : (n + 1) * TX, :] = rows


def shape(*dims):
    return jax.ShapeDtypeStruct(dims, F32)


def cost(flops, moved):
    return pl.CostEstimate(flops=flops, bytes_accessed=moved, transcendentals=0)


def on_device(adjoint_last, adjoint_prev, adjoint_source, sensor_cell, sound_class, depth_index):
    sensors = lax.axis_size("sensor")
    count_x, count_y = lax.axis_size("gx"), lax.axis_size("gy")
    params = pltpu.CompilerParams(vmem_limit_bytes=40 * 2**20)
    flat = (NZ * TX, TY)
    block = (TX, NZ, TY)
    p0, old, wc, near, far = pl.pallas_call(
        pack_kernel,
        out_shape=[shape(*block)] * 3 + [shape(2, NZ, TY)] * 2,
        in_specs=[VMEM] * 4,
        out_specs=[VMEM] * 5,
        compiler_params=params,
        name="pack_columns",
    )(adjoint_last.reshape(flat), adjoint_prev.reshape(flat), sound_class.reshape(flat), depth_index)
    far = lax.ppermute(far, "gy", swap_pairs(count_y, 1))
    near = lax.ppermute(near, "gy", swap_pairs(count_y, 0))
    padded = (TX, 2, DEEP, TY)
    strip_a, strip_b, aux_p, aux_o, aux_w = pl.pallas_call(
        edge_kernel,
        out_shape=[shape(STRIP, NZ, TY)] * 2 + [shape(*block)] * 3,
        in_specs=[VMEM] * 5 + [SMEM] * 2,
        out_specs=[VMEM] * 5,
        scratch_shapes=[pltpu.VMEM(padded, F32)] * 3,
        compiler_params=params,
        name="edge_rows",
    )(p0, old, wc, near, far, sensor_cell, adjoint_source)
    strip_a = lax.ppermute(strip_a, "gx", swap_pairs(count_x, 0))
    strip_b = lax.ppermute(strip_b, "gx", swap_pairs(count_x, 1))
    field, surface, trace = pl.pallas_call(
        steps_kernel,
        out_shape=[shape(*flat), shape(TX, TY), shape(sensors, STEPS * TX, TY)],
        in_specs=[VMEM] * 9 + [SMEM] * 2,
        out_specs=[VMEM] * 3,
        scratch_shapes=[
            pltpu.VMEM((3, ROWS, 2, DEEP, TY), F32),
            pltpu.VMEM((ROWS, 2, NZ, TY), F32),
            pltpu.VMEM((ROWS, TY), jnp.int32),
            pltpu.VMEM((STEPS, ROWS, TY), F32),
        ],
        compiler_params=params,
        name="six_steps",
    )(p0, old, wc, aux_p, aux_o, aux_w, strip_a, strip_b, depth_index, sensor_cell, adjoint_source)
    others = lax.all_to_all(trace, "sensor", 0, 0)
    gram = jnp.sum(trace[0][None] * others, axis=(1, 2)) / (STEPS * TX * TY)
    return field.reshape(1, NZ, TX, TY), surface[None], gram.reshape(1, 1, 1, sensors)


def solution(mesh):
    return jax.shard_map(
        on_device,
        mesh=mesh,
        in_specs=(
            P("sensor", None, "gx", "gy"),
            P("sensor", None, "gx", "gy"),
            P("sensor", None),
            P("sensor"),
            P(None, "gx", "gy"),
            P("gx", "gy"),
        ),
        out_specs=(
            P("sensor", None, "gx", "gy"),
            P("sensor", "gx", "gy"),
            P("gx", "gy", "sensor", None),
        ),
        check_vma=False,
    )
```

time: 201 us -> 72.5 us (0.36)
  the two profiles are of different devices: /device:TPU:486 before, /device:TPU:262 now
where the time goes in v1:
time: 72.5 us; the launch traced here: 72 us
  waiting for transfers between devices  25.9 us (36%)
  Pallas kernels  23.8 us (33%)
  starting transfers between devices  15 us (21%)
  local copies, waits for them, and re-layouts  5.28 us (7%)
  between operations  1.37 us (2%)
    pallas_call x1, Pallas kernels, on_device(): pl.pallas_call(steps_kernel, out_shape=[shape(*flat), shape(TX, TY), shap...  19.5 us
    ppermute x1, waiting for transfers between devices, on_device(): far = lax.ppermute(far, 'gy', swap_pairs(count_y, 1))  8 us
    all_to_all x1, waiting for transfers between devices, on_device(): others = lax.all_to_all(trace, 'sensor', 0, 0)  7.19 us
    ppermute x1, waiting for transfers between devices, on_device(): strip_b = lax.ppermute(strip_b, 'gx', swap_pairs(count_x, 1))  5.82 us
    ppermute x1, waiting for transfers between devices, on_device(): strip_a = lax.ppermute(strip_a, 'gx', swap_pairs(count_x, 0))  4.85 us
    unnamed x12, local copies, waits for them, and re-layouts  4.47 us
    ppermute x1, starting transfers between devices, on_device(): strip_b = lax.ppermute(strip_b, 'gx', swap_pairs(count_x, 1))  4.35 us
    ppermute x1, starting transfers between devices, on_device(): strip_a = lax.ppermute(strip_a, 'gx', swap_pairs(count_x, 0))  3.48 us
  transfers between devices with their start and end apart: 5, of which 4 were waited for; matrix products, arithmetic and copies ran while one was open for 1% of the time, Pallas kernels for 0%

profile of v1, /device:TPU:262, one launch (start us, length us, event | category | flops | bytes accessed | tf_op | source)
XLA Modules:
  0.0 72.0 jit_solution(17448121335460811231)
XLA Ops:
  0.6 0.0 copy-start
  0.6 1.0 %copy-done = f32[1,64,16,128]{3,2,1,0:T(8,128)S(1)} copy-done((f32[1,64,16,128]{3,2,1,0:T(8,128)S(1)}, f32[1,64,16,128]{3,2,1,0:T(8,128)}, u32[]{:S(2)}) %copy-start) | copy-done | bytes 524312
  1.7 1.0 %copy-done.1 = f32[1,64,16,128]{3,2,1,0:T(8,128)S(1)} copy-done((f32[1,64,16,128]{3,2,1,0:T(8,128)S(1)}, f32[1,64,16,128]{3,2,1,0:T(8,128)}, u32[]{:S(2)}) %copy-start.1) | copy-done | bytes 524312
  2.7 1.0 %copy-done.2 = s32[64,16,128]{2,1,0:T(8,128)S(1)} copy-done((s32[64,16,128]{2,1,0:T(8,128)S(1)}, s32[64,16,128]{2,1,0:T(8,128)}, u32[]{:S(2)}) %copy-start.2) | copy-done | bytes 524312
  3.8 0.7 copy-done.3
  4.5 1.3 %pack_columns.1 = (f32[16,64,128]{2,1,0:T(8,128)S(1)}, f32[16,64,128]{2,1,0:T(8,128)S(1)}, f32[16,64,128]{2,1,0:T(8,128)S(1)}, f32[2,64,128]{2,1,0:T(8,128)S(1)}, f32[2,64,128]{2,1,0:T(8,128)S(1)}) custom-call(f32[1024,128]{1,0:T(8,128)S(1)} %bitcast.9, f32[1024,128]{1,0:T(8,128)S(1)} %bitcast.10, s32[1024,128]{1,0:T(8,128)S(1)} %bitcast.11, ...), custom_call_target="tpu_custom_call" | custom-call | tf_op jit(solution)/shard_map/pack_columns/pallas_call | solution.py:294
  5.7 1.9 %collective-permute-start = (f32[2,64,128]{2,1,0:T(8,128)S(1)}, f32[2,64,128]{2,1,0:T(8,128)S(1)}, u32[]{:S(2)}, u32[]{:S(2)}) collective-permute-start(f32[2,64,128]{2,1,0:T(8,128)S(1)} %get-tuple-element.19), channel_id=1, source_target_pairs={{0,1},{1,0},{2,3},{3,2},{4,5},{5,4},{6,7},{7,6},{8,9},{9,8},{10,11... | collective-permute-start | bytes 196616 | tf_op jit(solution)/shard_map/ppermute | solution.py:303
  7.7 1.9 %collective-permute-start.1 = (f32[2,64,128]{2,1,0:T(8,128)S(1)}, f32[2,64,128]{2,1,0:T(8,128)S(1)}, u32[]{:S(2)}, u32[]{:S(2)}) collective-permute-start(f32[2,64,128]{2,1,0:T(8,128)S(1)} %get-tuple-element.20), channel_id=1, source_target_pairs={{1,2},{2,1},{3,4},{4,3},{5,6},{6,5},{9,10},{10,9},{11,12},{12,11},... | collective-permute-start | bytes 196616 | tf_op jit(solution)/shard_map/ppermute | solution.py:302
  10.2 0.0 collective-permute-done.near
  10.2 8.0 %collective-permute-done.1.far = f32[2,64,128]{2,1,0:T(8,128)S(1)} collective-permute-done((f32[2,64,128]{2,1,0:T(8,128)S(1)}, f32[2,64,128]{2,1,0:T(8,128)S(1)}, u32[]{:S(2)}, u32[]{:S(2)}) %collective-permute-start.1) | collective-permute-done | bytes 65568 | tf_op jit(solution)/shard_map/ppermute | solution.py:302
  18.2 0.7 copy-done.5
  18.9 3.1 %edge_rows.1 = (f32[11,64,128]{2,1,0:T(8,128)S(1)}, f32[11,64,128]{2,1,0:T(8,128)S(1)}, f32[16,64,128]{2,1,0:T(8,128)S(1)}, f32[16,64,128]{2,1,0:T(8,128)S(1)}, f32[16,64,128]{2,1,0:T(8,128)S(1)}) custom-call(f32[16,64,128]{2,1,0:T(8,128)S(1)} %get-tuple-element.16.p0, f32[16,64,128]{2,1,0:T(8,128)S(1)} %get-tuple-element.17.old, ...), custom_call_target="tpu_custom_call" | custom-call | tf_op jit(solution)/shard_map/edge_rows/pallas_call | solution.py:305
  22.0 0.0 copy-start.4
  22.0 3.5 %collective-permute-start.2 = (f32[11,64,128]{2,1,0:T(8,128)S(1)}, f32[11,64,128]{2,1,0:T(8,128)S(1)}, u32[]{:S(2)}, u32[]{:S(2)}) collective-permute-start(f32[11,64,128]{2,1,0:T(8,128)S(1)} %get-tuple-element.24), channel_id=1, source_target_pairs={{0,8},{8,0},{16,24},{24,16},{32,40},{40,32},{48,56},{56,48},{64,72... | collective-permute-start | bytes 1081352 | tf_op jit(solution)/shard_map/ppermute | solution.py:314
  25.5 4.4 %collective-permute-start.3 = (f32[11,64,128]{2,1,0:T(8,128)S(1)}, f32[11,64,128]{2,1,0:T(8,128)S(1)}, u32[]{:S(2)}, u32[]{:S(2)}) collective-permute-start(f32[11,64,128]{2,1,0:T(8,128)S(1)} %get-tuple-element.25), channel_id=1, source_target_pairs={{8,16},{16,8},{24,32},{32,24},{40,48},{48,40},{56,64},{64,56},{72,... | collective-permute-start | bytes 1081352 | tf_op jit(solution)/shard_map/ppermute | solution.py:315
  29.8 4.8 %collective-permute-done.2.strip_a = f32[11,64,128]{2,1,0:T(8,128)S(1)} collective-permute-done((f32[11,64,128]{2,1,0:T(8,128)S(1)}, f32[11,64,128]{2,1,0:T(8,128)S(1)}, u32[]{:S(2)}, u32[]{:S(2)}) %collective-permute-start.2) | collective-permute-done | bytes 360480 | tf_op jit(solution)/shard_map/ppermute | solution.py:314
  34.7 5.8 %collective-permute-done.3.strip_b = f32[11,64,128]{2,1,0:T(8,128)S(1)} collective-permute-done((f32[11,64,128]{2,1,0:T(8,128)S(1)}, f32[11,64,128]{2,1,0:T(8,128)S(1)}, u32[]{:S(2)}, u32[]{:S(2)}) %collective-permute-start.3) | collective-permute-done | bytes 360480 | tf_op jit(solution)/shard_map/ppermute | solution.py:315
  40.5 0.0 copy-done.4
  40.5 19.5 %six_steps.1 = (f32[1024,128]{1,0:T(8,128)}, f32[16,128]{1,0:T(8,128)}, f32[4,96,128]{2,1,0:T(8,128)}) custom-call(f32[16,64,128]{2,1,0:T(8,128)S(1)} %get-tuple-element.16.p0, f32[16,64,128]{2,1,0:T(8,128)S(1)} %get-tuple-element.17.old, f32[16,64,128]{2,1,0:T(8,128)S(1)} %get-tuple-element.18.wc, f32[16,64,128]{2,1,0:T(8,128)S(1)} %get-tuple-element.21.aux_p, ...), custom_call_target="tpu_custom_call" | custom-call | tf_op jit(solution)/shard_map/six_steps/pallas_call | solution.py:316
  60.0 3.4 %all-to-all-start = ((f32[4,96,128]{2,1,0:T(8,128)}), f32[4,96,128]{2,1,0:T(8,128)S(1)}, u32[]{:S(2)}, u32[]{:S(2)}) async-start(f32[4,96,128]{2,1,0:T(8,128)} %get-tuple-element.28), calls=%async_computation | async-start | bytes 393216 | tf_op jit(solution)/shard_map/all_to_all | solution.py:330
  63.4 0.8 %slice_bitcast_fusion = f32[96,128]{1,0:T(8,128)S(1)} fusion(f32[4,96,128]{2,1,0:T(8,128)} %get-tuple-element.28), kind=kLoop, calls=%fused_computation.1 | loop fusion | bytes 98304 | tf_op jit(solution)/shard_map/mul | solution.py:331
  64.2 7.2 %all-to-all-done = f32[4,96,128]{2,1,0:T(8,128)S(1)} async-done(((f32[4,96,128]{2,1,0:T(8,128)}), f32[4,96,128]{2,1,0:T(8,128)S(1)}, u32[]{:S(2)}, u32[]{:S(2)}) %all-to-all-start) | async-done | bytes 196640 | tf_op jit(solution)/shard_map/all_to_all | solution.py:330
  71.3 0.1 multiply_reduce_fusion
  71.5 0.5 multiply_bitcast_fusion
  (4 shorter events, 0.0 us)
Async XLA Ops:
  0.6 1.0 %copy-start = (f32[1,64,16,128]{3,2,1,0:T(8,128)S(1)}, f32[1,64,16,128]{3,2,1,0:T(8,128)}, u32[]{:S(2)}) copy-start(f32[1,64,16,128]{3,2,1,0:T(8,128)} %param.6) | copy-start | bytes 1572868
  1.7 1.0 %copy-start.1 = (f32[1,64,16,128]{3,2,1,0:T(8,128)S(1)}, f32[1,64,16,128]{3,2,1,0:T(8,128)}, u32[]{:S(2)}) copy-start(f32[1,64,16,128]{3,2,1,0:T(8,128)} %param.7) | copy-start | bytes 1572868
  2.7 1.0 %copy-start.2 = (s32[64,16,128]{2,1,0:T(8,128)S(1)}, s32[64,16,128]{2,1,0:T(8,128)}, u32[]{:S(2)}) copy-start(s32[64,16,128]{2,1,0:T(8,128)} %param.10) | copy-start | bytes 1572868
  3.8 0.7 copy-start.3
  5.7 4.5 %collective-permute-start = (f32[2,64,128]{2,1,0:T(8,128)S(1)}, f32[2,64,128]{2,1,0:T(8,128)S(1)}, u32[]{:S(2)}, u32[]{:S(2)}) collective-permute-start(f32[2,64,128]{2,1,0:T(8,128)S(1)} %get-tuple-element.19), channel_id=1, source_target_pairs={{0,1},{1,0},{2,3},{3,2},{4,5},{5,4},{6,7},{7,6},{8,9},{9,8},{10,11... | collective-permute-start | bytes 196616 | tf_op jit(solution)/shard_map/ppermute | solution.py:303
  7.7 10.6 %collective-permute-start.1 = (f32[2,64,128]{2,1,0:T(8,128)S(1)}, f32[2,64,128]{2,1,0:T(8,128)S(1)}, u32[]{:S(2)}, u32[]{:S(2)}) collective-permute-start(f32[2,64,128]{2,1,0:T(8,128)S(1)} %get-tuple-element.20), channel_id=1, source_target_pairs={{1,2},{2,1},{3,4},{4,3},{5,6},{6,5},{9,10},{10,9},{11,12},{12,11},... | collective-permute-start | bytes 196616 | tf_op jit(solution)/shard_map/ppermute | solution.py:302
  18.2 0.7 copy-start.5
  22.0 18.5 %copy-start.4 = (s32[16,128]{1,0:T(8,128)S(1)}, s32[16,128]{1,0:T(8,128)}, u32[]{:S(2)}) copy-start(s32[16,128]{1,0:T(8,128)} %depth.3) | copy-start | bytes 24580
  22.0 12.7 %collective-permute-start.2 = (f32[11,64,128]{2,1,0:T(8,128)S(1)}, f32[11,64,128]{2,1,0:T(8,128)S(1)}, u32[]{:S(2)}, u32[]{:S(2)}) collective-permute-start(f32[11,64,128]{2,1,0:T(8,128)S(1)} %get-tuple-element.24), channel_id=1, source_target_pairs={{0,8},{8,0},{16,24},{24,16},{32,40},{40,32},{48,56},{56,48},{64,72... | collective-permute-start | bytes 1081352 | tf_op jit(solution)/shard_map/ppermute | solution.py:314
  25.5 15.0 %collective-permute-start.3 = (f32[11,64,128]{2,1,0:T(8,128)S(1)}, f32[11,64,128]{2,1,0:T(8,128)S(1)}, u32[]{:S(2)}, u32[]{:S(2)}) collective-permute-start(f32[11,64,128]{2,1,0:T(8,128)S(1)} %get-tuple-element.25), channel_id=1, source_target_pairs={{8,16},{16,8},{24,32},{32,24},{40,48},{48,40},{56,64},{64,56},{72,... | collective-permute-start | bytes 1081352 | tf_op jit(solution)/shard_map/ppermute | solution.py:315
  60.0 11.4 %all-to-all-start = ((f32[4,96,128]{2,1,0:T(8,128)}), f32[4,96,128]{2,1,0:T(8,128)S(1)}, u32[]{:S(2)}, u32[]{:S(2)}) async-start(f32[4,96,128]{2,1,0:T(8,128)} %get-tuple-element.28), calls=%async_computation | async-start | bytes 393216 | tf_op jit(solution)/shard_map/all_to_all | solution.py:330

commit v2 on v1

v2 whole, which is shorter than its diff:
```python
import functools

import jax
import jax.numpy as jnp
from jax import lax
from jax.experimental import pallas as pl
from jax.experimental.pallas import tpu as pltpu
from jax.sharding import PartitionSpec as P

STEPS = 6
COURANT_SQUARED = (0.08, 0.11, 0.14, 0.17, 0.2, 0.23, 0.26, 0.3)
SURFACE_RATE = 0.3

NZ, TX, TY = 64, 16, 128
HALO = 4
ROWS = TX + 2 * HALO
TOP = 8
DEEP = NZ + 16
CHUNK = 16
STRIP = 11
ITEMS = (("p0", 1), ("p0", 2), ("old", 1), ("p1", 2), ("p1", 3), ("p2", 3), ("wc", 1), ("wc", 2), ("p2", 4), ("wc", 3))
VMEM = pl.BlockSpec(memory_space=pltpu.VMEM)
SMEM = pl.BlockSpec(memory_space=pltpu.SMEM)
HBM = pl.BlockSpec(memory_space=pltpu.HBM)
F32 = jnp.float32


def lanes(rows):
    return lax.broadcasted_iota(jnp.int32, (rows, TY), 1)


def rolled(values, shift):
    shift = shift % TY
    return values if shift == 0 else pltpu.roll(values, shift, axis=1)


def swap_pairs(count, first):
    return [pair for i in range(first, count - 1, 2) for pair in ((i, i + 1), (i + 1, i))]


def pack_kernel(last, prev, kind, depth, p0, old, wc, near, far, depth_out, now_v, prev_v, kind_v, sems):
    copies = [
        pltpu.make_async_copy(src, dst, sems.at[i])
        for i, (src, dst) in enumerate(((last, now_v), (prev, prev_v), (kind, kind_v), (depth, depth_out)))
    ]
    for copy in copies:
        copy.start()
    even = lax.rem(lax.axis_index("gy"), 2) == 0
    lane = lanes(NZ)
    level = lax.broadcasted_iota(jnp.int32, (NZ, TY), 0)
    for copy in copies:
        copy.wait()

    def half(h, carry):
        left = jnp.zeros((NZ, TY), F32)
        right = jnp.zeros((NZ, TY), F32)
        for j in range(8):
            x = h * 8 + j
            here = pl.ds(x, NZ, stride=TX)
            now, before, k = now_v[here, :], prev_v[here, :], kind_v[here, :]
            coef = jnp.full((NZ, TY), COURANT_SQUARED[0], F32)
            for category in range(1, 8):
                coef = jnp.where(k == category, COURANT_SQUARED[category], coef)
            coef = jnp.where(level < depth_out[pl.ds(x, 1), :], coef, 0.0)
            p0[x], old[x], wc[x] = now, before, coef
            base = 16 * j
            for values, start, width in ((now, base, 6), (before, base + 6, 5), (coef, base + 11, 5)):
                mine = (lane >= start) & (lane < start + width)
                left = jnp.where(mine, rolled(values, start), left)
                right = jnp.where(mine, rolled(values, start - (TY - width)), right)
        near[h] = jnp.where(even, right, left)
        far[h] = jnp.where(even, left, right)
        return carry

    lax.fori_loop(0, 2, half, 0)


def update_row(now, old, wc, out, row, depth_row=None, trace=None, tiles=(0, 1)):
    lane = lanes(CHUNK)
    results = []
    total = jnp.zeros((8, TY), F32)
    for start in range(0, NZ, CHUNK):
        at = pl.ds(TOP + start, CHUNK)
        centre = [now[row, t, at, :] for t in (0, 1)]
        down = [pltpu.roll(c, 1, axis=1) for c in centre]
        up = [pltpu.roll(c, TY - 1, axis=1) for c in centre]
        for t in tiles:
            beside = jnp.where(lane == 0, down[1 - t], down[t]) + jnp.where(lane == TY - 1, up[1 - t], up[t])
            rows = now[row - 1, t, at, :] + now[row + 1, t, at, :]
            levels = now[row, t, pl.ds(TOP + start - 1, CHUNK), :] + now[row, t, pl.ds(TOP + start + 1, CHUNK), :]
            laplace = (rows + beside) + levels - 6.0 * centre[t]
            coef = wc[row, t, pl.ds(start, CHUNK), :]
            fresh = 2.0 * centre[t] - old[row, t, at, :] + coef * laplace
            fresh = jnp.where(coef > 0.0, fresh, 0.0)
            results.append((t, at, fresh))
            if t == 0 and depth_row is not None:
                level = lax.broadcasted_iota(jnp.int32, (CHUNK, TY), 0) + start
                bed = jnp.where(level == depth_row - 1, fresh, 0.0)
                for part in range(0, CHUNK, 8):
                    total = total + bed[part : part + 8]
    top = pl.ds(TOP - 1, 1)
    etas = []
    for t in tiles:
        eta = now[row, t, top, :]
        etas.append(eta + SURFACE_RATE * (results[t][2][0:1] - eta))
    for t, at, fresh in results:
        out[row, t, at, :] = fresh
    for t in tiles:
        out[row, t, top, :] = etas[t]
        out[row, t, TOP + NZ : TOP + NZ + 1, :] = jnp.zeros((1, TY), F32)
    if trace is not None:
        trace[row - HALO] = total


def fetch(source, source_s, sem):
    copy = pltpu.make_async_copy(source, source_s, sem)
    copy.start()
    return copy


def sensor_place(cell):
    number = cell[0]
    size_y = TY * lax.axis_size("gy")
    plane = TX * lax.axis_size("gx") * size_y
    z = lax.div(number, plane)
    x = lax.div(lax.rem(number, plane), size_y) - TX * lax.axis_index("gx")
    y = lax.rem(number, size_y) - TY * lax.axis_index("gy")
    tile = jnp.where((y >= 0) & (y < TY), 0, 1)
    lane = lax.rem(y + 2 * size_y, TY)
    return z, x, tile, lane, (y >= -5) & (y < TY + 5)


def inject(out, place, amount, first, end, depth, trace):
    z, x, tile, lane, here = place
    inner = jnp.minimum(x, TX - 1 - x)
    amount = jnp.where(here & (inner >= first) & (inner < end), amount, 0.0)
    hit = jnp.where(lanes(1) == lane, amount, 0.0)
    row = jnp.clip(x + HALO, 0, ROWS - 1)
    at = pl.ds(TOP + z, 1)
    out[row, tile, at, :] = out[row, tile, at, :] + hit
    top = pl.ds(TOP - 1, 1)
    out[row, tile, top, :] = out[row, tile, top, :] + jnp.where(z == 0, SURFACE_RATE, 0.0) * hit
    own = jnp.clip(x, 0, TX - 1)
    bed = (depth[pl.ds(own, 1), :] - 1 == z) & (tile == 0) & (inner >= 0)
    trace[own, 0:1, :] = trace[own, 0:1, :] + jnp.where(bed, hit, 0.0)


def own_rows(now, old, wc, out, first, end, depth, trace, tiles=(0, 1)):
    def pair(x, carry):
        for y in (x, TX - 1 - x):
            update_row(now, old, wc, out, y + HALO, depth[pl.ds(y, 1), :], trace, tiles)
        return carry

    lax.fori_loop(first, end, pair, 0)


def clear_ends(ref, row, t):
    ref[row, t, 0:TOP, :] = jnp.zeros((TOP, TY), F32)
    ref[row, t, TOP + NZ :, :] = jnp.zeros((8, TY), F32)


def edge_kernel(p0, old, wc, near, far, depth, cell, source, strip_a, strip_b, l0, lold, w, l1, l2, trace,
                source_s, sem):
    copy = fetch(source, source_s, sem)
    even = lax.rem(lax.axis_index("gy"), 2) == 0
    lane = lanes(NZ)
    body = slice(TOP, TOP + NZ)

    def half(h, carry):
        from_right = jnp.where(even, near[h], far[h])
        from_left = jnp.where(even, far[h], near[h])
        for j in range(8):
            x = h * 8 + j
            row = x + HALO
            base = 16 * j
            aux = []
            for start, width in ((base, 6), (base + 6, 5), (base + 11, 5)):
                right = rolled(from_right, -start)
                left = rolled(from_left, TY - width - start)
                aux.append(jnp.where(lane < width, right, jnp.where(lane >= TY - width, left, 0.0)))
            l0[row, 0, body, :], lold[row, 0, body, :], w[row, 0] = p0[x], old[x], wc[x]
            l0[row, 1, body, :], lold[row, 1, body, :], w[row, 1] = aux
            for t in (0, 1):
                clear_ends(l0, row, t)
        return carry

    lax.fori_loop(0, 2, half, 0)
    copy.wait()
    place = sensor_place(cell)
    own_rows(l0, lold, w, l1, 1, 5, depth, trace.at[0])
    inject(l1, place, source_s[0, 0], 1, 5, depth, trace.at[0])
    own_rows(l1, l0, w, l2, 2, 4, depth, trace.at[1])
    inject(l2, place, source_s[0, 1], 2, 4, depth, trace.at[1])

    upper_a = lax.rem(lax.axis_index("gx"), 2) == 0
    for strip, upper in ((strip_a, upper_a), (strip_b, ~upper_a)):
        corner = jnp.zeros((NZ, TY), F32)
        for k, (name, d) in enumerate(ITEMS):
            row = HALO + jnp.where(upper, TX - d, d - 1)
            if name == "wc":
                main, aux = w[row, 0], w[row, 1]
            else:
                ref = {"old": lold, "p0": l0, "p1": l1, "p2": l2}[name]
                main, aux = ref[row, 0, body, :], ref[row, 1, body, :]
            strip[k] = main
            if k < 8:
                corner = jnp.where((lane >= 16 * k) & (lane < 16 * k + 16), rolled(aux, 8 + 16 * k), corner)
        strip[STRIP - 1] = corner


def inner_kernel(l0, lold, w, l1_in, l2_in, trace_in, depth, cell, source, l1, l2, trace, l3, l4, l5, l6,
                 source_s, sem):
    copy = fetch(source, source_s, sem)
    copy.wait()
    place = sensor_place(cell)
    steps = [lold, l0, l1, l2, l3, l4, l5, l6]
    for n, first in zip(range(1, STEPS + 1), (5, 4, 3, 4, 5, 6)):
        now, old, out = steps[n], steps[n - 1], steps[n + 1]
        own_rows(now, old, w, out, first, TX // 2, depth, trace.at[n - 1], (0, 1) if n < STEPS else (0,))
        inject(out, place, source_s[0, n - 1], first, TX // 2, depth, trace.at[n - 1])


def frontier_kernel(l0_in, lold_in, w_in, l1_in, l2_in, l3_in, l4_in, l5_in, l6_in, trace_in, strip_a, strip_b, depth, cell, source,
                    l0, lold, w, l1, l2, l3, l4, l5, l6, trace, mine, others, source_s, sem):
    copy = fetch(source, source_s, sem)
    body = slice(TOP, TOP + NZ)
    lane = lanes(NZ)
    top = slice(TOP - 1, TOP)
    upper_a = lax.rem(lax.axis_index("gx"), 2) == 0
    for strip, upper in ((strip_a, upper_a), (strip_b, ~upper_a)):
        corner = strip[STRIP - 1]
        for k, (name, d) in enumerate(ITEMS):
            row = jnp.where(upper, HALO + TX - 1 + d, HALO - d)
            if k < 8:
                aux = jnp.where((lane < 8) | (lane >= TY - 8), rolled(corner, -(8 + 16 * k)), 0.0)
            else:
                aux = jnp.zeros((NZ, TY), F32)
            for t, values in ((0, strip[k]), (1, aux)):
                if name == "wc":
                    w[row, t] = values
                    continue
                ref = {"old": lold, "p0": l0, "p1": l1, "p2": l2}[name]
                clear_ends(ref, row, t)
                ref[row, t, body, :] = values
                if name == "p1":
                    l1[row, t, top, :] = SURFACE_RATE * values[0:1]
                if name == "p2" and d == 3:
                    eta = l1[row, t, top, :]
                    l2[row, t, top, :] = eta + SURFACE_RATE * (values[0:1] - eta)
    copy.wait()
    place = sensor_place(cell)
    steps = [lold, l0, l1, l2, l3, l4, l5, l6]
    for n, reach in zip(range(1, STEPS + 1), (1, 2, 3, 2, 1, 0)):
        now, old, out = steps[n], steps[n - 1], steps[n + 1]
        own_rows(now, old, w, out, 0, n, depth, trace.at[n - 1], (0, 1) if n < STEPS else (0,))

        def halo_pair(d, carry):
            for row in (HALO - d, HALO + TX - 1 + d):
                update_row(now, old, w, out, row)
            return carry

        if reach:
            lax.fori_loop(1, reach + 1, halo_pair, 0)
        inject(out, place, source_s[0, n - 1], -reach, n, depth, trace.at[n - 1])
    for n in range(STEPS):
        rows = jnp.sum(trace[n], axis=1)
        mine[n * TX : (n + 1) * TX, :] = rows * (1.0 / (STEPS * TX * TY))
        for s in range(others.shape[0]):
            others[s, n * TX : (n + 1) * TX, :] = rows


def give_kernel(final, field, surface):
    def give(x, carry):
        field[pl.ds(x, NZ, stride=TX), :] = final[x + HALO, 0, TOP : TOP + NZ, :]
        surface[pl.ds(x, 1), :] = final[x + HALO, 0, TOP - 1 : TOP, :]
        return carry

    lax.fori_loop(0, TX, give, 0)


def shape(*dims):
    return jax.ShapeDtypeStruct(dims, F32)


def cost(rows, moved):
    return pl.CostEstimate(flops=rows * NZ * TY * 16, bytes_accessed=moved, transcendentals=0)


SMALL = [pltpu.SMEM((1, STEPS), F32), pltpu.SemaphoreType.DMA]


def on_device(adjoint_last, adjoint_prev, adjoint_source, sensor_cell, sound_class, depth_index):
    sensors = lax.axis_size("sensor")
    count_x, count_y = lax.axis_size("gx"), lax.axis_size("gy")
    params = pltpu.CompilerParams(vmem_limit_bytes=8 * 2**20)
    flat = (NZ * TX, TY)
    block = (TX, NZ, TY)
    fields = [a.reshape(flat) for a in (adjoint_last, adjoint_prev, sound_class)]
    fields = [pltpu.with_memory_space_constraint(a, pltpu.HBM) for a in (*fields, depth_index)]
    adjoint_source = pltpu.with_memory_space_constraint(adjoint_source, pltpu.HBM)
    p0, old, wc, near, far, depth = pl.pallas_call(
        pack_kernel,
        out_shape=[shape(*block)] * 3 + [shape(2, NZ, TY)] * 2 + [jax.ShapeDtypeStruct((TX, TY), jnp.int32)],
        in_specs=[HBM] * 4,
        out_specs=[VMEM] * 6,
        scratch_shapes=[pltpu.VMEM(flat, F32), pltpu.VMEM(flat, F32), pltpu.VMEM(flat, jnp.int32), pltpu.SemaphoreType.DMA((4,))],
        compiler_params=params,
        name="pack_columns",
    )(*fields)
    far = lax.ppermute(far, "gy", swap_pairs(count_y, 1))
    near = lax.ppermute(near, "gy", swap_pairs(count_y, 0))
    state = shape(ROWS, 2, DEEP, TY)
    sums = shape(STEPS, TX, 8, TY)
    strip_a, strip_b, l0, lold, w, l1, l2, trace = pl.pallas_call(
        edge_kernel,
        out_shape=[shape(STRIP, NZ, TY)] * 2 + [state] * 2 + [shape(ROWS, 2, NZ, TY)] + [state] * 2 + [sums],
        in_specs=[VMEM] * 6 + [SMEM, HBM],
        out_specs=[VMEM] * 8,
        scratch_shapes=SMALL,
        compiler_params=params,
        cost_estimate=cost(24, 10**6),
        name="edge_rows",
    )(p0, old, wc, near, far, depth, sensor_cell, adjoint_source)
    strip_a = lax.ppermute(strip_a, "gx", swap_pairs(count_x, 0))
    strip_b = lax.ppermute(strip_b, "gx", swap_pairs(count_x, 1))
    l1, l2, trace, l3, l4, l5, l6 = pl.pallas_call(
        inner_kernel,
        out_shape=[state] * 2 + [sums] + [state] * 4,
        in_specs=[VMEM] * 7 + [SMEM, HBM],
        out_specs=[VMEM] * 7,
        scratch_shapes=SMALL,
        input_output_aliases={3: 0, 4: 1, 5: 2},
        compiler_params=params,
        cost_estimate=cost(100, 10**6),
        name="inner_rows",
    )(l0, lold, w, l1, l2, trace, depth, sensor_cell, adjoint_source)
    held = [l0, lold, w, l1, l2, l3, l4, l5, l6, trace]
    given = pl.pallas_call(
        frontier_kernel,
        out_shape=[shape(*a.shape) for a in held] + [shape(STEPS * TX, TY), shape(sensors, STEPS * TX, TY)],
        in_specs=[VMEM] * 13 + [SMEM, HBM],
        out_specs=[VMEM] * 12,
        scratch_shapes=SMALL,
        input_output_aliases={i: i for i in range(10)},
        compiler_params=params,
        cost_estimate=cost(100, 10**6),
        name="frontier_rows",
    )(*held, strip_a, strip_b, depth, sensor_cell, adjoint_source)
    final, mine, others = given[8], given[10], given[11]
    others = lax.all_to_all(others, "sensor", 0, 0)
    field, surface = pl.pallas_call(
        give_kernel,
        out_shape=[shape(*flat), shape(TX, TY)],
        in_specs=[VMEM],
        out_specs=[VMEM] * 2,
        compiler_params=params,
        cost_estimate=cost(8, 10**6),
        name="field_rows",
    )(final)
    gram = jnp.sum(mine[None] * others, axis=(1, 2))
    return field.reshape(1, NZ, TX, TY), surface[None], gram.reshape(1, 1, 1, sensors)


def solution(mesh):
    return jax.shard_map(
        on_device,
        mesh=mesh,
        in_specs=(
            P("sensor", None, "gx", "gy"),
            P("sensor", None, "gx", "gy"),
            P("sensor", None),
            P("sensor"),
            P(None, "gx", "gy"),
            P("gx", "gy"),
        ),
        out_specs=(
            P("sensor", None, "gx", "gy"),
            P("sensor", "gx", "gy"),
            P("gx", "gy", "sensor", None),
        ),
        check_vma=False,
    )
```

time: 72.5 us -> 54.8 us (0.76)
  Pallas kernels: 23.8 us -> 15.8 us
  local copies, waits for them, and re-layouts: 5.28 us -> 0 us
  waiting for transfers between devices: 25.9 us -> 21.6 us
    pallas_call x2 -> x4, Pallas kernels: 22.5 us -> 13.1 us  [the longest x1 5.99 us: on_device(): pl.pallas_call(frontier_kernel, out_shape=[shape(*a.shape) for a in held]...]
    unnamed x12 -> x0, local copies, waits for them, and re-layouts: 4.47 us -> none
    ppermute x1, waiting for transfers between devices: 4.85 us -> 0.9 us  [on_device(): strip_a = lax.ppermute(strip_a, 'gx', swap_pairs(count_x, 0))]
    pallas_call x1, Pallas kernels: 1.27 us -> 2.65 us  [on_device(): pl.pallas_call(pack_kernel, out_shape=[shape(*block)] * 3 + [shape(2, NZ,...]
    mul x1 -> x0, local copies, waits for them, and re-layouts: 0.8 us -> none  [on_device(): gram = jnp.sum(trace[0][None] * others, axis=(1, 2)) / (STEPS * TX * TY)]
  transfers between devices with their start and end apart: 5 -> 5, of which waited for: 4 -> 4; matrix products, arithmetic and copies ran while one was open for 1% -> 0% of each run, Pallas kernels for 0% -> 9%
where the time goes in v2:
time: 54.8 us; the launch traced here: 54.5 us
  waiting for transfers between devices  21.6 us (39%)
  Pallas kernels  15.8 us (29%)
  starting transfers between devices  15.1 us (28%)
  between operations  1.36 us (2%)
  other arithmetic  0.63 us (1%)
    ppermute x1, waiting for transfers between devices, on_device(): far = lax.ppermute(far, 'gy', swap_pairs(count_y, 1))  8 us
    all_to_all x1, waiting for transfers between devices, on_device(): others = lax.all_to_all(others, 'sensor', 0, 0)  6.92 us
    pallas_call x1, Pallas kernels, on_device(): pl.pallas_call(frontier_kernel, out_shape=[shape(*a.shape) for a in held]...  5.99 us
    ppermute x1, waiting for transfers between devices, on_device(): strip_b = lax.ppermute(strip_b, 'gx', swap_pairs(count_x, 1))  5.82 us
    ppermute x1, starting transfers between devices, on_device(): strip_b = lax.ppermute(strip_b, 'gx', swap_pairs(count_x, 1))  4.35 us
    pallas_call x1, Pallas kernels, on_device(): pl.pallas_call(inner_kernel, out_shape=[state] * 2 + [sums] + [state] * 4...  3.94 us
    ppermute x1, starting transfers between devices, on_device(): strip_a = lax.ppermute(strip_a, 'gx', swap_pairs(count_x, 0))  3.48 us
    all_to_all x1, starting transfers between devices, on_device(): others = lax.all_to_all(others, 'sensor', 0, 0)  3.38 us
  transfers between devices with their start and end apart: 5, of which 4 were waited for; matrix products, arithmetic and copies ran while one was open for 0% of the time, Pallas kernels for 9%

profile of v2, /device:TPU:262, one launch (start us, length us, event | category | flops | bytes accessed | tf_op | source)
XLA Modules:
  0.0 54.5 jit_solution(110030321215110530)
XLA Ops:
  0.6 2.7 %pack_columns.1 = (f32[16,64,128]{2,1,0:T(8,128)S(1)}, f32[16,64,128]{2,1,0:T(8,128)S(1)}, f32[16,64,128]{2,1,0:T(8,128)S(1)}, f32[2,64,128]{2,1,0:T(8,128)S(1)}...) custom-call(f32[1024,128]{1,0:T(8,128)} %bitcast.6, f32[1024,128]{1,0:T(8,128)} %bitcast.7, s32[1024,128]{1,0:T(8,128)} %bitcast.8, ...), custom_call_target="tpu_custom_call" | custom-call | tf_op jit(solution)/shard_map/pack_columns/pallas_call | solution.py:301
  3.3 1.9 %collective-permute-start = (f32[2,64,128]{2,1,0:T(8,128)S(1)}, f32[2,64,128]{2,1,0:T(8,128)S(1)}, u32[]{:S(2)}, u32[]{:S(2)}) collective-permute-start(f32[2,64,128]{2,1,0:T(8,128)S(1)} %get-tuple-element.32), channel_id=1, source_target_pairs={{0,1},{1,0},{2,3},{3,2},{4,5},{5,4},{6,7},{7,6},{8,9},{9,8},{10,11... | collective-permute-start | bytes 196616 | tf_op jit(solution)/shard_map/ppermute | solution.py:311
  5.2 1.9 %collective-permute-start.1 = (f32[2,64,128]{2,1,0:T(8,128)S(1)}, f32[2,64,128]{2,1,0:T(8,128)S(1)}, u32[]{:S(2)}, u32[]{:S(2)}) collective-permute-start(f32[2,64,128]{2,1,0:T(8,128)S(1)} %get-tuple-element.33), channel_id=1, source_target_pairs={{1,2},{2,1},{3,4},{4,3},{5,6},{6,5},{9,10},{10,9},{11,12},{12,11},... | collective-permute-start | bytes 196616 | tf_op jit(solution)/shard_map/ppermute | solution.py:310
  7.8 0.0 collective-permute-done.near
  7.8 8.0 %collective-permute-done.1.far = f32[2,64,128]{2,1,0:T(8,128)S(1)} collective-permute-done((f32[2,64,128]{2,1,0:T(8,128)S(1)}, f32[2,64,128]{2,1,0:T(8,128)S(1)}, u32[]{:S(2)}, u32[]{:S(2)}) %collective-permute-start.1) | collective-permute-done | bytes 65568 | tf_op jit(solution)/shard_map/ppermute | solution.py:310
  15.8 2.1 %edge_rows.1 = (f32[11,64,128]{2,1,0:T(8,128)S(1)}, f32[11,64,128]{2,1,0:T(8,128)S(1)}, f32[24,2,80,128]{3,2,1,0:T(8,128)S(1)}, f32[24,2,80,128]{3,2,1,0:T(8,128...) custom-call(f32[16,64,128]{2,1,0:T(8,128)S(1)} %get-tuple-element.29, ...), custom_call_target="tpu_custom_call" | custom-call | flops 3145728 | bytes 1000000 | tf_op jit(solution)/shard_map/edge_rows/pallas_call | solution.py:314
  17.9 3.5 %collective-permute-start.2 = (f32[11,64,128]{2,1,0:T(8,128)S(1)}, f32[11,64,128]{2,1,0:T(8,128)S(1)}, u32[]{:S(2)}, u32[]{:S(2)}) collective-permute-start(f32[11,64,128]{2,1,0:T(8,128)S(1)} %get-tuple-element.48), channel_id=1, source_target_pairs={{0,8},{8,0},{16,24},{24,16},{32,40},{40,32},{48,56},{56,48},{64,72... | collective-permute-start | bytes 1081352 | tf_op jit(solution)/shard_map/ppermute | solution.py:324
  21.4 4.4 %collective-permute-start.3 = (f32[11,64,128]{2,1,0:T(8,128)S(1)}, f32[11,64,128]{2,1,0:T(8,128)S(1)}, u32[]{:S(2)}, u32[]{:S(2)}) collective-permute-start(f32[11,64,128]{2,1,0:T(8,128)S(1)} %get-tuple-element.49), channel_id=1, source_target_pairs={{8,16},{16,8},{24,32},{32,24},{40,48},{48,40},{56,64},{64,56},{72,... | collective-permute-start | bytes 1081352 | tf_op jit(solution)/shard_map/ppermute | solution.py:325
  25.8 3.9 %inner_rows.1 = (f32[24,2,80,128]{3,2,1,0:T(8,128)S(1)}, f32[24,2,80,128]{3,2,1,0:T(8,128)S(1)}, f32[6,16,8,128]{3,2,1,0:T(8,128)S(1)}, f32[24,2,80,128]{3,2,1,0...) custom-call(f32[24,2,80,128]{3,2,1,0:T(8,128)S(1)} %get-tuple-elemen, ...), custom_call_target="tpu_custom_call", output_to_operand_aliasing={{0}: (3, {}), {1}: (4, {}), {2}: (5, {})} | custom-call | flops 13107200 | bytes 1000000 | tf_op jit(solution)/shard_map/inner_rows/pallas_call | solution.py:326
  29.7 0.9 %collective-permute-done.2.strip_a = f32[11,64,128]{2,1,0:T(8,128)S(1)} collective-permute-done((f32[11,64,128]{2,1,0:T(8,128)S(1)}, f32[11,64,128]{2,1,0:T(8,128)S(1)}, u32[]{:S(2)}, u32[]{:S(2)}) %collective-permute-start.2) | collective-permute-done | bytes 360480 | tf_op jit(solution)/shard_map/ppermute | solution.py:324
  30.6 5.8 %collective-permute-done.3.strip_b = f32[11,64,128]{2,1,0:T(8,128)S(1)} collective-permute-done((f32[11,64,128]{2,1,0:T(8,128)S(1)}, f32[11,64,128]{2,1,0:T(8,128)S(1)}, u32[]{:S(2)}, u32[]{:S(2)}) %collective-permute-start.3) | collective-permute-done | bytes 360480 | tf_op jit(solution)/shard_map/ppermute | solution.py:325
  36.4 6.0 %frontier_rows.1 = (f32[24,2,80,128]{3,2,1,0:T(8,128)S(1)}, f32[24,2,80,128]{3,2,1,0:T(8,128)S(1)}, f32[24,2,64,128]{3,2,1,0:T(8,128)S(1)}, f32[24,2,80,128]{3,2...) custom-call(f32[24,2,80,128]{3,2,1,0:T(8,128)S(1)} %get-tuple-elemen, ...), custom_call_target="tpu_custom_call", output_to_operand_aliasing={{0}: (0, {}), {1}: (1, {}), {2}: (2, {}), {3}: (3, {}), {4}... | custom-call | flops 13107200 | bytes 1000000 | tf_op jit(solution)/shard_map/frontier_rows/pallas_call | solution.py:338
  42.4 3.4 %all-to-all-start = ((f32[4,96,128]{2,1,0:T(8,128)}), f32[4,96,128]{2,1,0:T(8,128)S(1)}, u32[]{:S(2)}, u32[]{:S(2)}) async-start(f32[4,96,128]{2,1,0:T(8,128)} %get-tuple-element.54), calls=%async_computation | async-start | bytes 393216 | tf_op jit(solution)/shard_map/all_to_all | solution.py:350
  45.8 1.1 %field_rows.1 = (f32[1024,128]{1,0:T(8,128)}, f32[16,128]{1,0:T(8,128)}) custom-call(f32[24,2,80,128]{3,2,1,0:T(8,128)S(1)} %get-tuple-element.50.final), custom_call_target="tpu_custom_call" | custom-call | flops 1048576 | bytes 1000000 | tf_op jit(solution)/shard_map/field_rows/pallas_call | solution.py:351
  46.9 6.9 %all-to-all-done = f32[4,96,128]{2,1,0:T(8,128)S(1)} async-done(((f32[4,96,128]{2,1,0:T(8,128)}), f32[4,96,128]{2,1,0:T(8,128)S(1)}, u32[]{:S(2)}, u32[]{:S(2)}) %all-to-all-start) | async-done | bytes 196640 | tf_op jit(solution)/shard_map/all_to_all | solution.py:350
  53.8 0.6 %multiply_reduce_fusion = f32[4]{0:T(128)} fusion(f32[4,96,128]{2,1,0:T(8,128)S(1)} %all-to-all-done, f32[96,128]{1,0:T(8,128)S(1)} %get-tuple-element.53), kind=kLoop, calls=%fused_computation | loop fusion | flops 98300 | bytes 245776 | tf_op jit(solution)/shard_map/reduce_sum | solution.py:360
Async XLA Ops:
  3.3 4.5 %collective-permute-start = (f32[2,64,128]{2,1,0:T(8,128)S(1)}, f32[2,64,128]{2,1,0:T(8,128)S(1)}, u32[]{:S(2)}, u32[]{:S(2)}) collective-permute-start(f32[2,64,128]{2,1,0:T(8,128)S(1)} %get-tuple-element.32), channel_id=1, source_target_pairs={{0,1},{1,0},{2,3},{3,2},{4,5},{5,4},{6,7},{7,6},{8,9},{9,8},{10,11... | collective-permute-start | bytes 196616 | tf_op jit(solution)/shard_map/ppermute | solution.py:311
  5.2 10.6 %collective-permute-start.1 = (f32[2,64,128]{2,1,0:T(8,128)S(1)}, f32[2,64,128]{2,1,0:T(8,128)S(1)}, u32[]{:S(2)}, u32[]{:S(2)}) collective-permute-start(f32[2,64,128]{2,1,0:T(8,128)S(1)} %get-tuple-element.33), channel_id=1, source_target_pairs={{1,2},{2,1},{3,4},{4,3},{5,6},{6,5},{9,10},{10,9},{11,12},{12,11},... | collective-permute-start | bytes 196616 | tf_op jit(solution)/shard_map/ppermute | solution.py:310
  17.9 12.7 %collective-permute-start.2 = (f32[11,64,128]{2,1,0:T(8,128)S(1)}, f32[11,64,128]{2,1,0:T(8,128)S(1)}, u32[]{:S(2)}, u32[]{:S(2)}) collective-permute-start(f32[11,64,128]{2,1,0:T(8,128)S(1)} %get-tuple-element.48), channel_id=1, source_target_pairs={{0,8},{8,0},{16,24},{24,16},{32,40},{40,32},{48,56},{56,48},{64,72... | collective-permute-start | bytes 1081352 | tf_op jit(solution)/shard_map/ppermute | solution.py:324
  21.4 15.0 %collective-permute-start.3 = (f32[11,64,128]{2,1,0:T(8,128)S(1)}, f32[11,64,128]{2,1,0:T(8,128)S(1)}, u32[]{:S(2)}, u32[]{:S(2)}) collective-permute-start(f32[11,64,128]{2,1,0:T(8,128)S(1)} %get-tuple-element.49), channel_id=1, source_target_pairs={{8,16},{16,8},{24,32},{32,24},{40,48},{48,40},{56,64},{64,56},{72,... | collective-permute-start | bytes 1081352 | tf_op jit(solution)/shard_map/ppermute | solution.py:325
  42.4 11.4 %all-to-all-start = ((f32[4,96,128]{2,1,0:T(8,128)}), f32[4,96,128]{2,1,0:T(8,128)S(1)}, u32[]{:S(2)}, u32[]{:S(2)}) async-start(f32[4,96,128]{2,1,0:T(8,128)} %get-tuple-element.54), calls=%async_computation | async-start | bytes 393216 | tf_op jit(solution)/shard_map/all_to_all | solution.py:350

commit v3 on v2

--- a/solution.py
+++ b/solution.py
@@ -38,18 +38,20 @@
     return [pair for i in range(first, count - 1, 2) for pair in ((i, i + 1), (i + 1, i))]
 
 
-def pack_kernel(last, prev, kind, depth, p0, old, wc, near, far, depth_out, now_v, prev_v, kind_v, sems):
+def pack_kernel(last, prev, kind, depth, p0, old, wc, far, near, depth_out, now_v, prev_v, kind_v, depth_v, sems):
     copies = [
         pltpu.make_async_copy(src, dst, sems.at[i])
-        for i, (src, dst) in enumerate(((last, now_v), (prev, prev_v), (kind, kind_v), (depth, depth_out)))
+        for i, (src, dst) in enumerate(((last, now_v), (prev, prev_v), (kind, kind_v), (depth, depth_v)))
     ]
     for copy in copies:
         copy.start()
     even = lax.rem(lax.axis_index("gy"), 2) == 0
     lane = lanes(NZ)
     level = lax.broadcasted_iota(jnp.int32, (NZ, TY), 0)
+    depth_out[...] = jnp.zeros((ROWS, TY), jnp.int32)
     for copy in copies:
         copy.wait()
+    depth_out[HALO : HALO + TX, :] = depth_v[...]
 
     def half(h, carry):
         left = jnp.zeros((NZ, TY), F32)
@@ -61,7 +63,7 @@
             coef = jnp.full((NZ, TY), COURANT_SQUARED[0], F32)
             for category in range(1, 8):
                 coef = jnp.where(k == category, COURANT_SQUARED[category], coef)
-            coef = jnp.where(level < depth_out[pl.ds(x, 1), :], coef, 0.0)
+            coef = jnp.where(level < depth_v[pl.ds(x, 1), :], coef, 0.0)
             p0[x], old[x], wc[x] = now, before, coef
             base = 16 * j
             for values, start, width in ((now, base, 6), (before, base + 6, 5), (coef, base + 11, 5)):
@@ -82,10 +84,10 @@
     for start in range(0, NZ, CHUNK):
         at = pl.ds(TOP + start, CHUNK)
         centre = [now[row, t, at, :] for t in (0, 1)]
-        down = [pltpu.roll(c, 1, axis=1) for c in centre]
-        up = [pltpu.roll(c, TY - 1, axis=1) for c in centre]
         for t in tiles:
-            beside = jnp.where(lane == 0, down[1 - t], down[t]) + jnp.where(lane == TY - 1, up[1 - t], up[t])
+            left = pltpu.roll(jnp.where(lane == TY - 1, centre[1 - t], centre[t]), 1, axis=1)
+            right = pltpu.roll(jnp.where(lane == 0, centre[1 - t], centre[t]), TY - 1, axis=1)
+            beside = left + right
             rows = now[row - 1, t, at, :] + now[row + 1, t, at, :]
             levels = now[row, t, pl.ds(TOP + start - 1, CHUNK), :] + now[row, t, pl.ds(TOP + start + 1, CHUNK), :]
             laplace = (rows + beside) + levels - 6.0 * centre[t]
@@ -109,7 +111,7 @@
         out[row, t, top, :] = etas[t]
         out[row, t, TOP + NZ : TOP + NZ + 1, :] = jnp.zeros((1, TY), F32)
     if trace is not None:
-        trace[row - HALO] = total
+        trace[row] = total
 
 
 def fetch(source, source_s, sem):
@@ -130,25 +132,27 @@
     return z, x, tile, lane, (y >= -5) & (y < TY + 5)
 
 
-def inject(out, place, amount, first, end, depth, trace):
+def inject(out, place, amount, inside, depth, trace):
     z, x, tile, lane, here = place
-    inner = jnp.minimum(x, TX - 1 - x)
-    amount = jnp.where(here & (inner >= first) & (inner < end), amount, 0.0)
-    hit = jnp.where(lanes(1) == lane, amount, 0.0)
+    hit = jnp.where(lanes(1) == lane, jnp.where(here & inside, amount, 0.0), 0.0)
     row = jnp.clip(x + HALO, 0, ROWS - 1)
     at = pl.ds(TOP + z, 1)
     out[row, tile, at, :] = out[row, tile, at, :] + hit
     top = pl.ds(TOP - 1, 1)
     out[row, tile, top, :] = out[row, tile, top, :] + jnp.where(z == 0, SURFACE_RATE, 0.0) * hit
-    own = jnp.clip(x, 0, TX - 1)
-    bed = (depth[pl.ds(own, 1), :] - 1 == z) & (tile == 0) & (inner >= 0)
-    trace[own, 0:1, :] = trace[own, 0:1, :] + jnp.where(bed, hit, 0.0)
+    bed = (depth[pl.ds(row, 1), :] - 1 == z) & (tile == 0)
+    trace[row, 0:1, :] = trace[row, 0:1, :] + jnp.where(bed, hit, 0.0)
+
+
+def between(x, first, end):
+    inner = jnp.minimum(x, TX - 1 - x)
+    return (inner >= first) & (inner < end)
 
 
 def own_rows(now, old, wc, out, first, end, depth, trace, tiles=(0, 1)):
     def pair(x, carry):
         for y in (x, TX - 1 - x):
-            update_row(now, old, wc, out, y + HALO, depth[pl.ds(y, 1), :], trace, tiles)
+            update_row(now, old, wc, out, y + HALO, depth[pl.ds(y + HALO, 1), :], trace, tiles)
         return carry
 
     lax.fori_loop(first, end, pair, 0)
@@ -159,7 +163,7 @@
     ref[row, t, TOP + NZ :, :] = jnp.zeros((8, TY), F32)
 
 
-def edge_kernel(p0, old, wc, near, far, depth, cell, source, strip_a, strip_b, l0, lold, w, l1, l2, trace,
+def edge_kernel(p0, old, wc, far, near, depth, cell, source, strip_a, strip_b, l0, lold, w, l1, l2, trace,
                 source_s, sem):
     copy = fetch(source, source_s, sem)
     even = lax.rem(lax.axis_index("gy"), 2) == 0
@@ -188,9 +192,9 @@
     copy.wait()
     place = sensor_place(cell)
     own_rows(l0, lold, w, l1, 1, 5, depth, trace.at[0])
-    inject(l1, place, source_s[0, 0], 1, 5, depth, trace.at[0])
+    inject(l1, place, source_s[0, 0], between(place[1], 1, 5), depth, trace.at[0])
     own_rows(l1, l0, w, l2, 2, 4, depth, trace.at[1])
-    inject(l2, place, source_s[0, 1], 2, 4, depth, trace.at[1])
+    inject(l2, place, source_s[0, 1], between(place[1], 2, 4), depth, trace.at[1])
 
     upper_a = lax.rem(lax.axis_index("gx"), 2) == 0
     for strip, upper in ((strip_a, upper_a), (strip_b, ~upper_a)):
@@ -217,56 +221,68 @@
     for n, first in zip(range(1, STEPS + 1), (5, 4, 3, 4, 5, 6)):
         now, old, out = steps[n], steps[n - 1], steps[n + 1]
         own_rows(now, old, w, out, first, TX // 2, depth, trace.at[n - 1], (0, 1) if n < STEPS else (0,))
-        inject(out, place, source_s[0, n - 1], first, TX // 2, depth, trace.at[n - 1])
-
-
-def frontier_kernel(l0_in, lold_in, w_in, l1_in, l2_in, l3_in, l4_in, l5_in, l6_in, trace_in, strip_a, strip_b, depth, cell, source,
-                    l0, lold, w, l1, l2, l3, l4, l5, l6, trace, mine, others, source_s, sem):
+        inject(out, place, source_s[0, n - 1], between(place[1], first, TX // 2), depth, trace.at[n - 1])
+
+
+def frontier_kernel(facing, last, *refs):
+    ins, rest = refs[:14], refs[14:]
+    strip, depth, cell, source = ins[10:]
+    l0, lold, w, l1, l2, l3, l4, l5, l6, trace = rest[:10]
+    source_s, sem = rest[-2:]
     copy = fetch(source, source_s, sem)
     body = slice(TOP, TOP + NZ)
     lane = lanes(NZ)
     top = slice(TOP - 1, TOP)
-    upper_a = lax.rem(lax.axis_index("gx"), 2) == 0
-    for strip, upper in ((strip_a, upper_a), (strip_b, ~upper_a)):
-        corner = strip[STRIP - 1]
-        for k, (name, d) in enumerate(ITEMS):
-            row = jnp.where(upper, HALO + TX - 1 + d, HALO - d)
-            if k < 8:
-                aux = jnp.where((lane < 8) | (lane >= TY - 8), rolled(corner, -(8 + 16 * k)), 0.0)
-            else:
-                aux = jnp.zeros((NZ, TY), F32)
-            for t, values in ((0, strip[k]), (1, aux)):
-                if name == "wc":
-                    w[row, t] = values
-                    continue
-                ref = {"old": lold, "p0": l0, "p1": l1, "p2": l2}[name]
-                clear_ends(ref, row, t)
-                ref[row, t, body, :] = values
-                if name == "p1":
-                    l1[row, t, top, :] = SURFACE_RATE * values[0:1]
-                if name == "p2" and d == 3:
-                    eta = l1[row, t, top, :]
-                    l2[row, t, top, :] = eta + SURFACE_RATE * (values[0:1] - eta)
+    upper = lax.rem(lax.axis_index("gx"), 2) == facing
+
+    first, step = jnp.where(upper, HALO + TX - 1, HALO), jnp.where(upper, -1, 1)
+
+    def place_of(i):
+        return first + step * i
+
+    corner = strip[STRIP - 1]
+    for k, (name, d) in enumerate(ITEMS):
+        row = place_of(-d)
+        if k < 8:
+            aux = jnp.where((lane < 8) | (lane >= TY - 8), rolled(corner, -(8 + 16 * k)), 0.0)
+        else:
+            aux = jnp.zeros((NZ, TY), F32)
+        for t, values in ((0, strip[k]), (1, aux)):
+            if name == "wc":
+                w[row, t] = values
+                continue
+            ref = {"old": lold, "p0": l0, "p1": l1, "p2": l2}[name]
+            clear_ends(ref, row, t)
+            ref[row, t, body, :] = values
+            if name == "p1":
+                l1[row, t, top, :] = SURFACE_RATE * values[0:1]
+            if name == "p2" and d == 3:
+                eta = l1[row, t, top, :]
+                l2[row, t, top, :] = eta + SURFACE_RATE * (values[0:1] - eta)
     copy.wait()
     place = sensor_place(cell)
+    x_s = jnp.where(upper, TX - 1 - place[1], place[1])
     steps = [lold, l0, l1, l2, l3, l4, l5, l6]
     for n, reach in zip(range(1, STEPS + 1), (1, 2, 3, 2, 1, 0)):
         now, old, out = steps[n], steps[n - 1], steps[n + 1]
-        own_rows(now, old, w, out, 0, n, depth, trace.at[n - 1], (0, 1) if n < STEPS else (0,))
-
-        def halo_pair(d, carry):
-            for row in (HALO - d, HALO + TX - 1 + d):
-                update_row(now, old, w, out, row)
+        half = (n + reach) // 2
+        tiles = (0, 1) if n < STEPS else (0,)
+
+        def pair(i, carry):
+            for j in (i - reach, i - reach + half):
+                row = place_of(j)
+                update_row(now, old, w, out, row, depth[pl.ds(row, 1), :], trace.at[n - 1], tiles)
             return carry
 
-        if reach:
-            lax.fori_loop(1, reach + 1, halo_pair, 0)
-        inject(out, place, source_s[0, n - 1], -reach, n, depth, trace.at[n - 1])
-    for n in range(STEPS):
-        rows = jnp.sum(trace[n], axis=1)
-        mine[n * TX : (n + 1) * TX, :] = rows * (1.0 / (STEPS * TX * TY))
-        for s in range(others.shape[0]):
-            others[s, n * TX : (n + 1) * TX, :] = rows
+        lax.fori_loop(0, half, pair, 0)
+        inject(out, place, source_s[0, n - 1], (x_s >= -reach) & (x_s < n), depth, trace.at[n - 1])
+    if last:
+        mine, others = rest[10:12]
+        for n in range(STEPS):
+            rows = jnp.sum(trace[n, HALO : HALO + TX], axis=1)
+            mine[n * TX : (n + 1) * TX, :] = rows * (1.0 / (STEPS * TX * TY))
+            for s in range(others.shape[0]):
+                others[s, n * TX : (n + 1) * TX, :] = rows
 
 
 def give_kernel(final, field, surface):
@@ -298,19 +314,21 @@
     fields = [a.reshape(flat) for a in (adjoint_last, adjoint_prev, sound_class)]
     fields = [pltpu.with_memory_space_constraint(a, pltpu.HBM) for a in (*fields, depth_index)]
     adjoint_source = pltpu.with_memory_space_constraint(adjoint_source, pltpu.HBM)
-    p0, old, wc, near, far, depth = pl.pallas_call(
+    p0, old, wc, far, near, depth = pl.pallas_call(
         pack_kernel,
-        out_shape=[shape(*block)] * 3 + [shape(2, NZ, TY)] * 2 + [jax.ShapeDtypeStruct((TX, TY), jnp.int32)],
+        out_shape=[shape(*block)] * 3 + [shape(2, NZ, TY)] * 2 + [jax.ShapeDtypeStruct((ROWS, TY), jnp.int32)],
         in_specs=[HBM] * 4,
         out_specs=[VMEM] * 6,
-        scratch_shapes=[pltpu.VMEM(flat, F32), pltpu.VMEM(flat, F32), pltpu.VMEM(flat, jnp.int32), pltpu.SemaphoreType.DMA((4,))],
+        scratch_shapes=[pltpu.VMEM(flat, F32), pltpu.VMEM(flat, F32), pltpu.VMEM(flat, jnp.int32),
+            pltpu.VMEM((TX, TY), jnp.int32), pltpu.SemaphoreType.DMA((4,)),
+        ],
         compiler_params=params,
         name="pack_columns",
     )(*fields)
     far = lax.ppermute(far, "gy", swap_pairs(count_y, 1))
     near = lax.ppermute(near, "gy", swap_pairs(count_y, 0))
     state = shape(ROWS, 2, DEEP, TY)
-    sums = shape(STEPS, TX, 8, TY)
+    sums = shape(STEPS, ROWS, 8, TY)
     strip_a, strip_b, l0, lold, w, l1, l2, trace = pl.pallas_call(
         edge_kernel,
         out_shape=[shape(STRIP, NZ, TY)] * 2 + [state] * 2 + [shape(ROWS, 2, NZ, TY)] + [state] * 2 + [sums],
@@ -320,7 +338,7 @@
         compiler_params=params,
         cost_estimate=cost(24, 10**6),
         name="edge_rows",
-    )(p0, old, wc, near, far, depth, sensor_cell, adjoint_source)
+    )(p0, old, wc, far, near, depth, sensor_cell, adjoint_source)
     strip_a = lax.ppermute(strip_a, "gx", swap_pairs(count_x, 0))
     strip_b = lax.ppermute(strip_b, "gx", swap_pairs(count_x, 1))
     l1, l2, trace, l3, l4, l5, l6 = pl.pallas_call(
@@ -335,18 +353,20 @@
         name="inner_rows",
     )(l0, lold, w, l1, l2, trace, depth, sensor_cell, adjoint_source)
     held = [l0, lold, w, l1, l2, l3, l4, l5, l6, trace]
-    given = pl.pallas_call(
-        frontier_kernel,
-        out_shape=[shape(*a.shape) for a in held] + [shape(STEPS * TX, TY), shape(sensors, STEPS * TX, TY)],
-        in_specs=[VMEM] * 13 + [SMEM, HBM],
-        out_specs=[VMEM] * 12,
-        scratch_shapes=SMALL,
-        input_output_aliases={i: i for i in range(10)},
-        compiler_params=params,
-        cost_estimate=cost(100, 10**6),
-        name="frontier_rows",
-    )(*held, strip_a, strip_b, depth, sensor_cell, adjoint_source)
-    final, mine, others = given[8], given[10], given[11]
+    for facing, strip in enumerate((strip_a, strip_b)):
+        ends = [shape(STEPS * TX, TY), shape(sensors, STEPS * TX, TY)] if facing else []
+        held = pl.pallas_call(
+            functools.partial(frontier_kernel, facing, bool(facing)),
+            out_shape=[shape(*a.shape) for a in held] + ends,
+            in_specs=[VMEM] * 12 + [SMEM, HBM],
+            out_specs=[VMEM] * (10 + len(ends)),
+            scratch_shapes=SMALL,
+            input_output_aliases={i: i for i in range(10)},
+            compiler_params=params,
+            cost_estimate=cost(60, 10**6),
+            name="frontier_" + "ab"[facing],
+        )(*held, strip, depth, sensor_cell, adjoint_source)
+    final, mine, others = held[8], held[10], held[11]
     others = lax.all_to_all(others, "sensor", 0, 0)
     field, surface = pl.pallas_call(
         give_kernel,

time: 54.8 us -> 52.4 us (0.956)
  the two profiles are of different devices: /device:TPU:262 before, /device:TPU:6 now
where the time goes in v3:
time: 52.4 us; the launch traced here: 52.1 us
  starting transfers between devices  24.9 us (48%)
  Pallas kernels  15.8 us (30%)
  waiting for transfers between devices  9.45 us (18%)
  between operations  1.36 us (3%)
  other arithmetic  0.63 us (1%)
    ppermute x1, starting transfers between devices, on_device(): near = lax.ppermute(near, 'gy', swap_pairs(count_y, 0))  10.5 us
    pallas_call x2, Pallas kernels, on_device(): pl.pallas_call(functools.partial(frontier_kernel, facing, bool(facing)),...  6.37 us
    all_to_all x1, starting transfers between devices, on_device(): others = lax.all_to_all(others, 'sensor', 0, 0)  5.91 us
    all_to_all x1, waiting for transfers between devices, on_device(): others = lax.all_to_all(others, 'sensor', 0, 0)  5.66 us
    ppermute x1, starting transfers between devices, on_device(): strip_b = lax.ppermute(strip_b, 'gx', swap_pairs(count_x, 1))  4.35 us
    pallas_call x1, Pallas kernels, on_device(): pl.pallas_call(inner_kernel, out_shape=[state] * 2 + [sums] + [state] * 4...  3.66 us
    ppermute x1, starting transfers between devices, on_device(): strip_a = lax.ppermute(strip_a, 'gx', swap_pairs(count_x, 0))  3.48 us
    pallas_call x1, Pallas kernels, on_device(): pl.pallas_call(pack_kernel, out_shape=[shape(*block)] * 3 + [shape(2, NZ,...  2.66 us
  transfers between devices with their start and end apart: 5, of which 4 were waited for; matrix products, arithmetic and copies ran while one was open for 0% of the time, Pallas kernels for 14%

profile of v3, /device:TPU:6, one launch (start us, length us, event | category | flops | bytes accessed | tf_op | source)
XLA Modules:
  0.0 52.1 jit_solution(2361245724246081221)
XLA Ops:
  0.6 2.7 %pack_columns.1 = (f32[16,64,128]{2,1,0:T(8,128)S(1)}, f32[16,64,128]{2,1,0:T(8,128)S(1)}, f32[16,64,128]{2,1,0:T(8,128)S(1)}, f32[2,64,128]{2,1,0:T(8,128)S(1)}...) custom-call(f32[1024,128]{1,0:T(8,128)} %bitcast.6, f32[1024,128]{1,0:T(8,128)} %bitcast.7, s32[1024,128]{1,0:T(8,128)} %bitcast.8, ...), custom_call_target="tpu_custom_call" | custom-call | tf_op jit(solution)/shard_map/pack_columns/pallas_call | solution.py:317
  3.3 0.7 %collective-permute-start = (f32[2,64,128]{2,1,0:T(8,128)S(1)}, f32[2,64,128]{2,1,0:T(8,128)S(1)}, u32[]{:S(2)}, u32[]{:S(2)}) collective-permute-start(f32[2,64,128]{2,1,0:T(8,128)S(1)} %get-tuple-element.42), channel_id=1, source_target_pairs={{1,2},{2,1},{3,4},{4,3},{5,6},{6,5},{9,10},{10,9},{11,12},{12,11},... | collective-permute-start | bytes 196616 | tf_op jit(solution)/shard_map/ppermute | solution.py:328
  4.0 10.5 %collective-permute-start.1 = (f32[2,64,128]{2,1,0:T(8,128)S(1)}, f32[2,64,128]{2,1,0:T(8,128)S(1)}, u32[]{:S(2)}, u32[]{:S(2)}) collective-permute-start(f32[2,64,128]{2,1,0:T(8,128)S(1)} %get-tuple-element.43), channel_id=1, source_target_pairs={{0,1},{1,0},{2,3},{3,2},{4,5},{5,4},{6,7},{7,6},{8,9},{9,8},{10,11... | collective-permute-start | bytes 196616 | tf_op jit(solution)/shard_map/ppermute | solution.py:329
  15.1 0.0 collective-permute-done.far
  15.1 0.2 collective-permute-done.1.near
  15.3 2.0 %edge_rows.1 = (f32[11,64,128]{2,1,0:T(8,128)S(1)}, f32[11,64,128]{2,1,0:T(8,128)S(1)}, f32[24,2,80,128]{3,2,1,0:T(8,128)S(1)}, f32[24,2,80,128]{3,2,1,0:T(8,128...) custom-call(f32[16,64,128]{2,1,0:T(8,128)S(1)} %get-tuple-element.39, ...), custom_call_target="tpu_custom_call" | custom-call | flops 3145728 | bytes 1000000 | tf_op jit(solution)/shard_map/edge_rows/pallas_call | solution.py:332
  17.4 3.5 %collective-permute-start.2 = (f32[11,64,128]{2,1,0:T(8,128)S(1)}, f32[11,64,128]{2,1,0:T(8,128)S(1)}, u32[]{:S(2)}, u32[]{:S(2)}) collective-permute-start(f32[11,64,128]{2,1,0:T(8,128)S(1)} %get-tuple-element.58), channel_id=1, source_target_pairs={{0,8},{8,0},{16,24},{24,16},{32,40},{40,32},{48,56},{56,48},{64,72... | collective-permute-start | bytes 1081352 | tf_op jit(solution)/shard_map/ppermute | solution.py:342
  20.8 4.4 %collective-permute-start.3 = (f32[11,64,128]{2,1,0:T(8,128)S(1)}, f32[11,64,128]{2,1,0:T(8,128)S(1)}, u32[]{:S(2)}, u32[]{:S(2)}) collective-permute-start(f32[11,64,128]{2,1,0:T(8,128)S(1)} %get-tuple-element.69), channel_id=1, source_target_pairs={{8,16},{16,8},{24,32},{32,24},{40,48},{48,40},{56,64},{64,56},{72,... | collective-permute-start | bytes 1081352 | tf_op jit(solution)/shard_map/ppermute | solution.py:343
  25.2 3.7 %inner_rows.1 = (f32[24,2,80,128]{3,2,1,0:T(8,128)S(1)}, f32[24,2,80,128]{3,2,1,0:T(8,128)S(1)}, f32[6,24,8,128]{3,2,1,0:T(8,128)S(1)}, f32[24,2,80,128]{3,2,1,0...) custom-call(f32[24,2,80,128]{3,2,1,0:T(8,128)S(1)} %get-tuple-elemen, ...), custom_call_target="tpu_custom_call", output_to_operand_aliasing={{0}: (3, {}), {1}: (4, {}), {2}: (5, {})} | custom-call | flops 13107200 | bytes 1000000 | tf_op jit(solution)/shard_map/inner_rows/pallas_call | solution.py:344
  28.9 1.0 %collective-permute-done.2.refs_10_ = f32[11,64,128]{2,1,0:T(8,128)S(1)} collective-permute-done((f32[11,64,128]{2,1,0:T(8,128)S(1)}, f32[11,64,128]{2,1,0:T(8,128)S(1)}, u32[]{:S(2)}, u32[]{:S(2)}) %collective-permute-start.2) | collective-permute-done | bytes 360480 | tf_op jit(solution)/shard_map/ppermute | solution.py:342
  29.9 2.8 %frontier_a.1 = (f32[24,2,80,128]{3,2,1,0:T(8,128)S(1)}, f32[24,2,80,128]{3,2,1,0:T(8,128)S(1)}, f32[24,2,64,128]{3,2,1,0:T(8,128)S(1)}, f32[24,2,80,128]{3,2,1,...) custom-call(f32[24,2,80,128]{3,2,1,0:T(8,128)S(1)} %get-tuple-elemen, ...), custom_call_target="tpu_custom_call", output_to_operand_aliasing={{0}: (0, {}), {1}: (1, {}), {2}: (2, {}), {3}: (3, {}), {4}... | custom-call | flops 7864320 | bytes 1000000 | tf_op jit(solution)/shard_map/frontier_a/pallas_call | solution.py:358
  32.7 2.5 %collective-permute-done.3.refs_10_ = f32[11,64,128]{2,1,0:T(8,128)S(1)} collective-permute-done((f32[11,64,128]{2,1,0:T(8,128)S(1)}, f32[11,64,128]{2,1,0:T(8,128)S(1)}, u32[]{:S(2)}, u32[]{:S(2)}) %collective-permute-start.3) | collective-permute-done | bytes 360480 | tf_op jit(solution)/shard_map/ppermute | solution.py:343
  35.2 3.6 %frontier_b.1 = (f32[24,2,80,128]{3,2,1,0:T(8,128)S(1)}, f32[24,2,80,128]{3,2,1,0:T(8,128)S(1)}, f32[24,2,64,128]{3,2,1,0:T(8,128)S(1)}, f32[24,2,80,128]{3,2,1,...) custom-call(f32[24,2,80,128]{3,2,1,0:T(8,128)S(1)} %get-tuple-elemen, ...), custom_call_target="tpu_custom_call", output_to_operand_aliasing={{0}: (0, {}), {1}: (1, {}), {2}: (2, {}), {3}: (3, {}), {4}... | custom-call | flops 7864320 | bytes 1000000 | tf_op jit(solution)/shard_map/frontier_b/pallas_call | solution.py:358
  38.8 5.9 %all-to-all-start = ((f32[4,96,128]{2,1,0:T(8,128)}), f32[4,96,128]{2,1,0:T(8,128)S(1)}, u32[]{:S(2)}, u32[]{:S(2)}) async-start(f32[4,96,128]{2,1,0:T(8,128)} %get-tuple-element.74), calls=%async_computation | async-start | bytes 393216 | tf_op jit(solution)/shard_map/all_to_all | solution.py:370
  44.7 1.1 %field_rows.1 = (f32[1024,128]{1,0:T(8,128)}, f32[16,128]{1,0:T(8,128)}) custom-call(f32[24,2,80,128]{3,2,1,0:T(8,128)S(1)} %get-tuple-element.70.final), custom_call_target="tpu_custom_call" | custom-call | flops 1048576 | bytes 1000000 | tf_op jit(solution)/shard_map/field_rows/pallas_call | solution.py:371
  45.8 5.7 %all-to-all-done = f32[4,96,128]{2,1,0:T(8,128)S(1)} async-done(((f32[4,96,128]{2,1,0:T(8,128)}), f32[4,96,128]{2,1,0:T(8,128)S(1)}, u32[]{:S(2)}, u32[]{:S(2)}) %all-to-all-start) | async-done | bytes 196640 | tf_op jit(solution)/shard_map/all_to_all | solution.py:370
  51.5 0.6 %multiply_reduce_fusion = f32[4]{0:T(128)} fusion(f32[4,96,128]{2,1,0:T(8,128)S(1)} %all-to-all-done, f32[96,128]{1,0:T(8,128)S(1)} %get-tuple-element.73), kind=kLoop, calls=%fused_computation | loop fusion | flops 98300 | bytes 245776 | tf_op jit(solution)/shard_map/reduce_sum | solution.py:380
Async XLA Ops:
  3.3 11.8 %collective-permute-start = (f32[2,64,128]{2,1,0:T(8,128)S(1)}, f32[2,64,128]{2,1,0:T(8,128)S(1)}, u32[]{:S(2)}, u32[]{:S(2)}) collective-permute-start(f32[2,64,128]{2,1,0:T(8,128)S(1)} %get-tuple-element.42), channel_id=1, source_target_pairs={{1,2},{2,1},{3,4},{4,3},{5,6},{6,5},{9,10},{10,9},{11,12},{12,11},... | collective-permute-start | bytes 196616 | tf_op jit(solution)/shard_map/ppermute | solution.py:328
  4.0 11.3 %collective-permute-start.1 = (f32[2,64,128]{2,1,0:T(8,128)S(1)}, f32[2,64,128]{2,1,0:T(8,128)S(1)}, u32[]{:S(2)}, u32[]{:S(2)}) collective-permute-start(f32[2,64,128]{2,1,0:T(8,128)S(1)} %get-tuple-element.43), channel_id=1, source_target_pairs={{0,1},{1,0},{2,3},{3,2},{4,5},{5,4},{6,7},{7,6},{8,9},{9,8},{10,11... | collective-permute-start | bytes 196616 | tf_op jit(solution)/shard_map/ppermute | solution.py:329
  17.4 12.6 %collective-permute-start.2 = (f32[11,64,128]{2,1,0:T(8,128)S(1)}, f32[11,64,128]{2,1,0:T(8,128)S(1)}, u32[]{:S(2)}, u32[]{:S(2)}) collective-permute-start(f32[11,64,128]{2,1,0:T(8,128)S(1)} %get-tuple-element.58), channel_id=1, source_target_pairs={{0,8},{8,0},{16,24},{24,16},{32,40},{40,32},{48,56},{56,48},{64,72... | collective-permute-start | bytes 1081352 | tf_op jit(solution)/shard_map/ppermute | solution.py:342
  20.8 14.4 %collective-permute-start.3 = (f32[11,64,128]{2,1,0:T(8,128)S(1)}, f32[11,64,128]{2,1,0:T(8,128)S(1)}, u32[]{:S(2)}, u32[]{:S(2)}) collective-permute-start(f32[11,64,128]{2,1,0:T(8,128)S(1)} %get-tuple-element.69), channel_id=1, source_target_pairs={{8,16},{16,8},{24,32},{32,24},{40,48},{48,40},{56,64},{64,56},{72,... | collective-permute-start | bytes 1081352 | tf_op jit(solution)/shard_map/ppermute | solution.py:343
  38.8 12.6 %all-to-all-start = ((f32[4,96,128]{2,1,0:T(8,128)}), f32[4,96,128]{2,1,0:T(8,128)S(1)}, u32[]{:S(2)}, u32[]{:S(2)}) async-start(f32[4,96,128]{2,1,0:T(8,128)} %get-tuple-element.74), calls=%async_computation | async-start | bytes 393216 | tf_op jit(solution)/shard_map/all_to_all | solution.py:370

commit v4 on v3

v4 whole, which is shorter than its diff:
```python
import functools

import jax
import jax.numpy as jnp
from jax import lax
from jax.experimental import pallas as pl
from jax.experimental.pallas import tpu as pltpu
from jax.sharding import PartitionSpec as P

STEPS = 6
COURANT_SQUARED = (0.08, 0.11, 0.14, 0.17, 0.2, 0.23, 0.26, 0.3)
SURFACE_RATE = 0.3

NZ, TX, TY = 64, 16, 128
HALO = 4
ROWS = TX + 2 * HALO
TOP = 8
DEEP = NZ + 16
CHUNK = 16
STRIP = 11
ITEMS = (("p0", 1), ("p0", 2), ("old", 1), ("p1", 2), ("p1", 3), ("p2", 3), ("wc", 1), ("wc", 2), ("p2", 4), ("wc", 3))
VMEM = pl.BlockSpec(memory_space=pltpu.VMEM)
SMEM = pl.BlockSpec(memory_space=pltpu.SMEM)
HBM = pl.BlockSpec(memory_space=pltpu.HBM)
F32 = jnp.float32


def lanes(rows):
    return lax.broadcasted_iota(jnp.int32, (rows, TY), 1)


def rolled(values, shift):
    shift = shift % TY
    return values if shift == 0 else pltpu.roll(values, shift, axis=1)


def swap_pairs(count, first):
    return [pair for i in range(first, count - 1, 2) for pair in ((i, i + 1), (i + 1, i))]


def clear_ends(ref, row, t):
    ref[row, t, 0:TOP, :] = jnp.zeros((TOP, TY), F32)
    ref[row, t, TOP + NZ :, :] = jnp.zeros((8, TY), F32)


PLACES = ((0, 6), (6, 5), (11, 5))


def pack_kernel(last, prev, kind, depth, source, far, near, l0, lold, w, depth_out, amounts,
                now_v, prev_v, kind_v, depth_v, source_v, sems):
    part = NZ // 2
    copies = [pltpu.make_async_copy(depth, depth_v, sems.at[0])]
    for z in (0, 1):
        at = pl.ds(z * part * TX, part * TX)
        for src, dst in ((last, now_v), (prev, prev_v), (kind, kind_v)):
            copies.append(pltpu.make_async_copy(src.at[at], dst.at[at], sems.at[len(copies)]))
    copies.append(pltpu.make_async_copy(source, source_v, sems.at[len(copies)]))
    for copy in copies:
        copy.start()
    even = lax.rem(lax.axis_index("gy"), 2) == 0
    lane = lanes(part)
    spot = lax.rem(lane, 16)
    depth_out[...] = jnp.zeros((ROWS, TY), jnp.int32)
    for x in range(TX):
        for t in (0, 1):
            clear_ends(l0, x + HALO, t)
    copies[0].wait()
    depth_out[HALO : HALO + TX, :] = depth_v[...]
    copies[7].wait()
    amounts[...] = jnp.zeros((8, TY), F32)
    for n in range(STEPS):
        amounts[n : n + 1, :] = jnp.broadcast_to(source_v[0:1, n : n + 1], (1, TY))
    for z in (0, 1):
        for copy in copies[1 + 3 * z : 4 + 3 * z]:
            copy.wait()
        start = z * part
        level = lax.broadcasted_iota(jnp.int32, (part, TY), 0) + start
        for h in (0, 1):
            groups = [jnp.zeros((part, TY), F32)] * 3
            for j in range(8):
                x = h * 8 + j
                here = pl.ds(x + start * TX, part, stride=TX)
                now, before, k = now_v[here, :], prev_v[here, :], kind_v[here, :]
                coef = jnp.full((part, TY), COURANT_SQUARED[0], F32)
                for category in range(1, 8):
                    coef = jnp.where(k == category, COURANT_SQUARED[category], coef)
                coef = jnp.where(level < depth_v[x : x + 1, :], coef, 0.0)
                l0[x + HALO, 0, TOP + start : TOP + start + part, :] = now
                lold[x + HALO, 0, TOP + start : TOP + start + part, :] = before
                w[x + HALO, 0, start : start + part, :] = coef
                for i, (values, (offset, width)) in enumerate(zip((now, before, coef), PLACES)):
                    middle = 16 * j + offset
                    if middle < width:
                        mask = (lane >= TY + middle - width) | (lane < middle + width)
                    else:
                        mask = (lane >= middle - width) & (lane < middle + width)
                    groups[i] = jnp.where(mask, rolled(values, middle), groups[i])
            left = jnp.where(spot < 6, groups[0], jnp.where(spot < 11, groups[1], groups[2]))
            moved = [rolled(group, width) for group, (_, width) in zip(groups, PLACES)]
            right = jnp.where(spot < 6, moved[0], jnp.where(spot < 11, moved[1], moved[2]))
            near[h, start : start + part, :] = jnp.where(even, right, left)
            far[h, start : start + part, :] = jnp.where(even, left, right)


def update_row(now, old, wc, out, row, depth_row=None, trace=None, tiles=(0, 1)):
    lane = lanes(CHUNK)
    results = []
    total = jnp.zeros((8, TY), F32)
    for start in range(0, NZ, CHUNK):
        at = pl.ds(TOP + start, CHUNK)
        centre = [now[row, t, at, :] for t in (0, 1)]
        for t in tiles:
            left = pltpu.roll(jnp.where(lane == TY - 1, centre[1 - t], centre[t]), 1, axis=1)
            right = pltpu.roll(jnp.where(lane == 0, centre[1 - t], centre[t]), TY - 1, axis=1)
            beside = left + right
            rows = now[row - 1, t, at, :] + now[row + 1, t, at, :]
            levels = now[row, t, pl.ds(TOP + start - 1, CHUNK), :] + now[row, t, pl.ds(TOP + start + 1, CHUNK), :]
            laplace = (rows + beside) + levels - 6.0 * centre[t]
            coef = wc[row, t, pl.ds(start, CHUNK), :]
            fresh = 2.0 * centre[t] - old[row, t, at, :] + coef * laplace
            fresh = jnp.where(coef > 0.0, fresh, 0.0)
            results.append((t, at, fresh))
            if t == 0 and depth_row is not None:
                level = lax.broadcasted_iota(jnp.int32, (CHUNK, TY), 0) + start
                bed = jnp.where(level == depth_row - 1, fresh, 0.0)
                for part in range(0, CHUNK, 8):
                    total = total + bed[part : part + 8]
    top = pl.ds(TOP - 1, 1)
    etas = []
    for t in tiles:
        eta = now[row, t, top, :]
        etas.append(eta + SURFACE_RATE * (results[t][2][0:1] - eta))
    for t, at, fresh in results:
        out[row, t, at, :] = fresh
    for t in tiles:
        out[row, t, top, :] = etas[t]
        out[row, t, TOP + NZ : TOP + NZ + 1, :] = jnp.zeros((1, TY), F32)
    if trace is not None:
        trace[row - HALO : row - HALO + 1, :] = jnp.sum(total, axis=0, keepdims=True)


def sensor_place(cell):
    number = cell[0]
    size_y = TY * lax.axis_size("gy")
    plane = TX * lax.axis_size("gx") * size_y
    z = lax.div(number, plane)
    x = lax.div(lax.rem(number, plane), size_y) - TX * lax.axis_index("gx")
    y = lax.rem(number, size_y) - TY * lax.axis_index("gy")
    tile = jnp.where((y >= 0) & (y < TY), 0, 1)
    lane = lax.rem(y + 2 * size_y, TY)
    return z, x, tile, lane, (y >= -5) & (y < TY + 5)


def inject(out, place, amount, inside, depth, trace):
    z, x, tile, lane, here = place
    hit = jnp.where((lanes(1) == lane) & here & inside, amount, 0.0)
    row = jnp.clip(x + HALO, 0, ROWS - 1)
    at = pl.ds(TOP + z, 1)
    out[row, tile, at, :] = out[row, tile, at, :] + hit
    top = pl.ds(TOP - 1, 1)
    out[row, tile, top, :] = out[row, tile, top, :] + jnp.where(z == 0, SURFACE_RATE, 0.0) * hit
    bed = (depth[pl.ds(row, 1), :] - 1 == z) & (tile == 0) & (x >= 0) & (x < TX)
    at = pl.ds(jnp.clip(x, 0, TX - 1), 1)
    trace[at, :] = trace[at, :] + jnp.where(bed, hit, 0.0)


def between(x, first, end):
    inner = jnp.minimum(x, TX - 1 - x)
    return (inner >= first) & (inner < end)


def own_rows(now, old, wc, out, first, end, depth, trace, tiles=(0, 1)):
    for x in range(first, end):
        for row in (x + HALO, TX - 1 - x + HALO):
            update_row(now, old, wc, out, row, depth[row : row + 1, :], trace, tiles)


def unpack(far, near, l0, lold, w, wanted):
    even = lax.rem(lax.axis_index("gy"), 2) == 0
    lane = lanes(NZ)
    spot = lax.rem(lane, 16)
    body = slice(TOP, TOP + NZ)
    for h in (0, 1):
        right = jnp.where(even, near[h], far[h])
        left = jnp.where(even, far[h], near[h])
        left_6, left_5 = rolled(left, -6), rolled(left, -5)
        merged = (
            jnp.where(spot >= 10, left_6, right),
            jnp.where(spot < 6, left_5, right),
            jnp.where(spot < 11, left_5, right),
        )
        for j in range(8):
            if h * 8 + j not in wanted:
                continue
            row = h * 8 + j + HALO
            aux = [
                jnp.where((lane < width) | (lane >= TY - width), rolled(values, -(16 * j + offset)), 0.0)
                for values, (offset, width) in zip(merged, PLACES)
            ]
            l0[row, 1, body, :], lold[row, 1, body, :], w[row, 1] = aux


def edge_kernel(far, near, l0_in, lold_in, w_in, depth, source, cell, strip_a, strip_b, l0, lold, w, l1, l2, trace):
    lane = lanes(NZ)
    body = slice(TOP, TOP + NZ)
    unpack(far, near, l0, lold, w, [*range(6), *range(10, TX)])
    place = sensor_place(cell)
    own_rows(l0, lold, w, l1, 1, 5, depth, trace.at[0])
    inject(l1, place, source[0:1, :], between(place[1], 1, 5), depth, trace.at[0])
    own_rows(l1, l0, w, l2, 2, 4, depth, trace.at[1])
    inject(l2, place, source[1:2, :], between(place[1], 2, 4), depth, trace.at[1])

    upper_a = lax.rem(lax.axis_index("gx"), 2) == 0
    for strip, upper in ((strip_a, upper_a), (strip_b, ~upper_a)):
        corner = jnp.zeros((NZ, TY), F32)
        for k, (name, d) in enumerate(ITEMS):
            row = HALO + jnp.where(upper, TX - d, d - 1)
            if name == "wc":
                main, aux = w[row, 0], w[row, 1]
            else:
                ref = {"old": lold, "p0": l0, "p1": l1, "p2": l2}[name]
                main, aux = ref[row, 0, body, :], ref[row, 1, body, :]
            strip[k] = main
            if k < 8:
                corner = jnp.where((lane >= 16 * k) & (lane < 16 * k + 16), rolled(aux, 8 + 16 * k), corner)
        strip[STRIP - 1] = corner


def inner_kernel(l0_in, lold_in, w_in, l1_in, l2_in, trace_in, far, near, depth, source, cell,
                 l0, lold, w, l1, l2, trace, l3, l4, l5, l6):
    unpack(far, near, l0, lold, w, range(6, 10))
    place = sensor_place(cell)
    steps = [lold, l0, l1, l2, l3, l4, l5, l6]
    for n, first in zip(range(1, STEPS + 1), (5, 4, 3, 4, 5, 6)):
        now, old, out = steps[n], steps[n - 1], steps[n + 1]
        own_rows(now, old, w, out, first, TX // 2, depth, trace.at[n - 1], (0, 1) if n < STEPS else (0,))
        inject(out, place, source[n - 1 : n, :], between(place[1], first, TX // 2), depth, trace.at[n - 1])


def frontier_kernel(facing, *refs):
    upper = lax.rem(lax.axis_index("gx"), 2) == facing

    @pl.when(upper)
    def _():
        frontier_side(True, *refs)

    @pl.when(~upper)
    def _():
        frontier_side(False, *refs)


def frontier_side(upper, *refs):
    strip, depth, source, cell = refs[10:14]
    l0, lold, w, l1, l2, l3, l4, l5, l6, trace, *others = refs[14:]
    body = slice(TOP, TOP + NZ)
    lane = lanes(NZ)
    top = slice(TOP - 1, TOP)

    def place_of(i):
        return HALO + (TX - 1 - i if upper else i)

    corner = strip[STRIP - 1]
    for k, (name, d) in enumerate(ITEMS):
        row = place_of(-d)
        if k < 8:
            aux = jnp.where((lane < 8) | (lane >= TY - 8), rolled(corner, -(8 + 16 * k)), 0.0)
        else:
            aux = jnp.zeros((NZ, TY), F32)
        for t, values in ((0, strip[k]), (1, aux)):
            if name == "wc":
                w[row, t] = values
                continue
            ref = {"old": lold, "p0": l0, "p1": l1, "p2": l2}[name]
            clear_ends(ref, row, t)
            ref[row, t, body, :] = values
            if name == "p1":
                l1[row, t, top, :] = SURFACE_RATE * values[0:1]
            if name == "p2" and d == 3:
                eta = l1[row, t, top, :]
                l2[row, t, top, :] = eta + SURFACE_RATE * (values[0:1] - eta)
    place = sensor_place(cell)
    x_s = TX - 1 - place[1] if upper else place[1]
    steps = [lold, l0, l1, l2, l3, l4, l5, l6]
    for n, reach in zip(range(1, STEPS + 1), (1, 2, 3, 2, 1, 0)):
        now, old, out = steps[n], steps[n - 1], steps[n + 1]
        for i in range(-reach, n):
            row = place_of(i)
            if i < 0:
                update_row(now, old, w, out, row)
            else:
                tiles = (0, 1) if n < STEPS else (0,)
                update_row(now, old, w, out, row, depth[row : row + 1, :], trace.at[n - 1], tiles)
        inject(out, place, source[n - 1 : n, :], (x_s >= -reach) & (x_s < n), depth, trace.at[n - 1])
    if others:
        for n in range(STEPS):
            scaled = trace[n] * (1.0 / (STEPS * TX * TY))
            for s in range(others[0].shape[0]):
                others[0][s, n * TX : (n + 1) * TX, :] = scaled


def give_kernel(final, field, surface):
    def give(x, carry):
        field[pl.ds(x, NZ, stride=TX), :] = final[x + HALO, 0, TOP : TOP + NZ, :]
        surface[pl.ds(x, 1), :] = final[x + HALO, 0, TOP - 1 : TOP, :]
        return carry

    lax.fori_loop(0, TX, give, 0)


def shape(*dims):
    return jax.ShapeDtypeStruct(dims, F32)


def cost(rows, moved):
    return pl.CostEstimate(flops=rows * NZ * TY * 16, bytes_accessed=moved, transcendentals=0)


def on_device(adjoint_last, adjoint_prev, adjoint_source, sensor_cell, sound_class, depth_index):
    sensors = lax.axis_size("sensor")
    count_x, count_y = lax.axis_size("gx"), lax.axis_size("gy")
    params = pltpu.CompilerParams(vmem_limit_bytes=8 * 2**20)
    flat = (NZ * TX, TY)
    block = (TX, NZ, TY)
    fields = [a.reshape(flat) for a in (adjoint_last, adjoint_prev, sound_class)]
    fields = [pltpu.with_memory_space_constraint(a, pltpu.HBM) for a in (*fields, depth_index, adjoint_source)]
    state = shape(ROWS, 2, DEEP, TY)
    sums = shape(STEPS, TX, TY)
    coefs = shape(ROWS, 2, NZ, TY)
    far, near, l0, lold, w, depth, amounts = pl.pallas_call(
        pack_kernel,
        out_shape=[shape(2, NZ, TY)] * 2 + [state] * 2 + [coefs, jax.ShapeDtypeStruct((ROWS, TY), jnp.int32), shape(8, TY)],
        in_specs=[HBM] * 5,
        out_specs=[VMEM] * 7,
        scratch_shapes=[
            pltpu.VMEM(flat, F32), pltpu.VMEM(flat, F32), pltpu.VMEM(flat, jnp.int32),
            pltpu.VMEM((TX, TY), jnp.int32), pltpu.VMEM((1, STEPS), F32), pltpu.SemaphoreType.DMA((8,)),
        ],
        compiler_params=params,
        name="pack_columns",
    )(*fields)
    far = lax.ppermute(far, "gy", swap_pairs(count_y, 1))
    near = lax.ppermute(near, "gy", swap_pairs(count_y, 0))
    strip_a, strip_b, l0, lold, w, l1, l2, trace = pl.pallas_call(
        edge_kernel,
        out_shape=[shape(STRIP, NZ, TY)] * 2 + [state] * 2 + [coefs] + [state] * 2 + [sums],
        in_specs=[VMEM] * 7 + [SMEM],
        out_specs=[VMEM] * 8,
        input_output_aliases={2: 2, 3: 3, 4: 4},
        compiler_params=params,
        cost_estimate=cost(24, 10**6),
        name="edge_rows",
    )(far, near, l0, lold, w, depth, amounts, sensor_cell)
    strip_b = lax.ppermute(strip_b, "gx", swap_pairs(count_x, 1))
    strip_a = lax.ppermute(strip_a, "gx", swap_pairs(count_x, 0))
    l0, lold, w, l1, l2, trace, l3, l4, l5, l6 = pl.pallas_call(
        inner_kernel,
        out_shape=[state] * 2 + [coefs] + [state] * 2 + [sums] + [state] * 4,
        in_specs=[VMEM] * 10 + [SMEM],
        out_specs=[VMEM] * 10,
        input_output_aliases={i: i for i in range(6)},
        compiler_params=params,
        cost_estimate=cost(100, 10**6),
        name="inner_rows",
    )(l0, lold, w, l1, l2, trace, far, near, depth, amounts, sensor_cell)
    held = [l0, lold, w, l1, l2, l3, l4, l5, l6, trace]
    for facing, strip in ((1, strip_b), (0, strip_a)):
        ends = [] if facing else [shape(sensors, STEPS * TX, TY)]
        held = pl.pallas_call(
            functools.partial(frontier_kernel, facing),
            out_shape=[shape(*a.shape) for a in held] + ends,
            in_specs=[VMEM] * 13 + [SMEM],
            out_specs=[VMEM] * (10 + len(ends)),
            input_output_aliases={i: i for i in range(10)},
            compiler_params=params,
            cost_estimate=cost(60, 10**6),
            name="frontier_" + "ab"[facing],
        )(*held, strip, depth, amounts, sensor_cell)
    final, mine = held[8], held[9].reshape(STEPS * TX, TY)
    others = lax.all_to_all(held[10], "sensor", 0, 0)
    field, surface = pl.pallas_call(
        give_kernel,
        out_shape=[shape(*flat), shape(TX, TY)],
        in_specs=[VMEM],
        out_specs=[VMEM] * 2,
        compiler_params=params,
        cost_estimate=cost(8, 10**6),
        name="field_rows",
    )(final)
    gram = jnp.sum(mine[None] * others, axis=(1, 2))
    return field.reshape(1, NZ, TX, TY), surface[None], gram.reshape(1, 1, 1, sensors)


def solution(mesh):
    return jax.shard_map(
        on_device,
        mesh=mesh,
        in_specs=(
            P("sensor", None, "gx", "gy"),
            P("sensor", None, "gx", "gy"),
            P("sensor", None),
            P("sensor"),
            P(None, "gx", "gy"),
            P("gx", "gy"),
        ),
        out_specs=(
            P("sensor", None, "gx", "gy"),
            P("sensor", "gx", "gy"),
            P("gx", "gy", "sensor", None),
        ),
        check_vma=False,
    )
```

time: 52.4 us -> 49.6 us (0.947)
  Pallas kernels: 15.8 us -> 10.6 us
  waiting for transfers between devices: 9.45 us -> 12.6 us
  starting transfers between devices: 24.9 us -> 24.1 us
    pallas_call x4, Pallas kernels: 12.7 us -> 8.3 us  [the longest x2 3.7 us: on_device(): pl.pallas_call(functools.partial(frontier_kernel, facing), out_shape=[sha...]
    ppermute x1, waiting for transfers between devices: 2.52 us -> 5.43 us  [on_device(): strip_b = lax.ppermute(strip_b, 'gx', swap_pairs(count_x, 1))]
    ppermute x1, starting transfers between devices: 3.48 us -> 1.92 us  [on_device(): strip_a = lax.ppermute(strip_a, 'gx', swap_pairs(count_x, 0))]
    pallas_call x1, Pallas kernels: 2.03 us -> 1.2 us  [on_device(): pl.pallas_call(edge_kernel, out_shape=[shape(STRIP, NZ, TY)] * 2 + [state...]
    ppermute x1, starting transfers between devices: 4.35 us -> 5.19 us  [on_device(): strip_b = lax.ppermute(strip_b, 'gx', swap_pairs(count_x, 1))]
  transfers between devices with their start and end apart: 5 -> 5, of which waited for: 4 -> 4; matrix products, arithmetic and copies ran while one was open for 0% -> 0% of each run, Pallas kernels for 14% -> 9%
where the time goes in v4:
time: 49.6 us; the launch traced here: 49.3 us
  starting transfers between devices  24.1 us (49%)
  waiting for transfers between devices  12.6 us (25%)
  Pallas kernels  10.6 us (21%)
  between operations  1.35 us (3%)
  other arithmetic  0.63 us (1%)
    ppermute x1, starting transfers between devices, on_device(): near = lax.ppermute(near, 'gy', swap_pairs(count_y, 0))  10.5 us
    all_to_all x1, starting transfers between devices, on_device(): others = lax.all_to_all(held[10], 'sensor', 0, 0)  5.89 us
    all_to_all x1, waiting for transfers between devices, on_device(): others = lax.all_to_all(held[10], 'sensor', 0, 0)  5.66 us
    ppermute x1, waiting for transfers between devices, on_device(): strip_b = lax.ppermute(strip_b, 'gx', swap_pairs(count_x, 1))  5.43 us
    ppermute x1, starting transfers between devices, on_device(): strip_b = lax.ppermute(strip_b, 'gx', swap_pairs(count_x, 1))  5.19 us
    pallas_call x2, Pallas kernels, on_device(): pl.pallas_call(functools.partial(frontier_kernel, facing), out_shape=[sha...  3.7 us
    pallas_call x1, Pallas kernels, on_device(): pl.pallas_call(pack_kernel, out_shape=[shape(2, NZ, TY)] * 2 + [state] *...  2.48 us
    pallas_call x1, Pallas kernels, on_device(): pl.pallas_call(inner_kernel, out_shape=[state] * 2 + [coefs] + [state] *...  2.11 us
  transfers between devices with their start and end apart: 5, of which 4 were waited for; matrix products, arithmetic and copies ran while one was open for 0% of the time, Pallas kernels for 9%

profile of v4, /device:TPU:6, one launch (start us, length us, event | category | flops | bytes accessed | tf_op | source)
XLA Modules:
  0.0 49.3 jit_solution(11809051199009288545)
XLA Ops:
  0.6 2.5 %pack_columns.1 = (f32[2,64,128]{2,1,0:T(8,128)S(1)}, f32[2,64,128]{2,1,0:T(8,128)S(1)}, f32[24,2,80,128]{3,2,1,0:T(8,128)S(1)}, f32[24,2,80,128]{3,2,1,0:T(8,12...) custom-call(f32[1024,128]{1,0:T(8,128)} %bitcast.8, f32[1024,128]{1,0:T(8,128)} %bitcast.9, ...), custom_call_target="tpu_custom_call" | custom-call | tf_op jit(solution)/shard_map/pack_columns/pallas_call | solution.py:329
  3.1 0.7 %collective-permute-start = (f32[2,64,128]{2,1,0:T(8,128)S(1)}, f32[2,64,128]{2,1,0:T(8,128)S(1)}, u32[]{:S(2)}, u32[]{:S(2)}) collective-permute-start(f32[2,64,128]{2,1,0:T(8,128)S(1)} %get-tuple-element.43), channel_id=1, source_target_pairs={{1,2},{2,1},{3,4},{4,3},{5,6},{6,5},{9,10},{10,9},{11,12},{12,11},... | collective-permute-start | bytes 196616 | tf_op jit(solution)/shard_map/ppermute | solution.py:341
  3.8 10.5 %collective-permute-start.1 = (f32[2,64,128]{2,1,0:T(8,128)S(1)}, f32[2,64,128]{2,1,0:T(8,128)S(1)}, u32[]{:S(2)}, u32[]{:S(2)}) collective-permute-start(f32[2,64,128]{2,1,0:T(8,128)S(1)} %get-tuple-element.44), channel_id=1, source_target_pairs={{0,1},{1,0},{2,3},{3,2},{4,5},{5,4},{6,7},{7,6},{8,9},{9,8},{10,11... | collective-permute-start | bytes 196616 | tf_op jit(solution)/shard_map/ppermute | solution.py:342
  14.9 0.0 collective-permute-done.far
  14.9 0.2 collective-permute-done.1.near
  15.1 1.2 %edge_rows.1 = (f32[11,64,128]{2,1,0:T(8,128)S(1)}, f32[11,64,128]{2,1,0:T(8,128)S(1)}, f32[24,2,80,128]{3,2,1,0:T(8,128)S(1)}, f32[24,2,80,128]{3,2,1,0:T(8,128...) custom-call(f32[2,64,128]{2,1,0:T(8,128)S(1)} %collective-permute-do, ...), custom_call_target="tpu_custom_call", output_to_operand_aliasing={{2}: (2, {}), {3}: (3, {}), {4}: (4, {})} | custom-call | flops 3145728 | bytes 1000000 | tf_op jit(solution)/shard_map/edge_rows/pallas_call | solution.py:343
  16.3 5.2 %collective-permute-start.2 = (f32[11,64,128]{2,1,0:T(8,128)S(1)}, f32[11,64,128]{2,1,0:T(8,128)S(1)}, u32[]{:S(2)}, u32[]{:S(2)}) collective-permute-start(f32[11,64,128]{2,1,0:T(8,128)S(1)} %get-tuple-element.66), channel_id=1, source_target_pairs={{8,16},{16,8},{24,32},{32,24},{40,48},{48,40},{56,64},{64,56},{72,... | collective-permute-start | bytes 1081352 | tf_op jit(solution)/shard_map/ppermute | solution.py:353
  21.5 1.9 %collective-permute-start.3 = (f32[11,64,128]{2,1,0:T(8,128)S(1)}, f32[11,64,128]{2,1,0:T(8,128)S(1)}, u32[]{:S(2)}, u32[]{:S(2)}) collective-permute-start(f32[11,64,128]{2,1,0:T(8,128)S(1)} %get-tuple-element.77), channel_id=1, source_target_pairs={{0,8},{8,0},{16,24},{24,16},{32,40},{40,32},{48,56},{56,48},{64,72... | collective-permute-start | bytes 1081352 | tf_op jit(solution)/shard_map/ppermute | solution.py:354
  23.5 2.1 %inner_rows.1 = (f32[24,2,80,128]{3,2,1,0:T(8,128)S(1)}, f32[24,2,80,128]{3,2,1,0:T(8,128)S(1)}, f32[24,2,64,128]{3,2,1,0:T(8,128)S(1)}, f32[24,2,80,128]{3,2,1,...) custom-call(f32[24,2,80,128]{3,2,1,0:T(8,128)S(1)} %get-tuple-elemen, ...), custom_call_target="tpu_custom_call", output_to_operand_aliasing={{0}: (0, {}), {1}: (1, {}), {2}: (2, {}), {3}: (3, {}), {4}... | custom-call | flops 13107200 | bytes 1000000 | tf_op jit(solution)/shard_map/inner_rows/pallas_call | solution.py:355
  25.6 5.4 %collective-permute-done.2.refs_10_ = f32[11,64,128]{2,1,0:T(8,128)S(1)} collective-permute-done((f32[11,64,128]{2,1,0:T(8,128)S(1)}, f32[11,64,128]{2,1,0:T(8,128)S(1)}, u32[]{:S(2)}, u32[]{:S(2)}) %collective-permute-start.2) | collective-permute-done | bytes 360480 | tf_op jit(solution)/shard_map/ppermute | solution.py:353
  31.0 1.5 %frontier_b.1 = (f32[24,2,80,128]{3,2,1,0:T(8,128)S(1)}, f32[24,2,80,128]{3,2,1,0:T(8,128)S(1)}, f32[24,2,64,128]{3,2,1,0:T(8,128)S(1)}, f32[24,2,80,128]{3,2,1,...) custom-call(f32[24,2,80,128]{3,2,1,0:T(8,128)S(1)} %get-tuple-elemen, ...), custom_call_target="tpu_custom_call", output_to_operand_aliasing={{0}: (0, {}), {1}: (1, {}), {2}: (2, {}), {3}: (3, {}), {4}... | custom-call | flops 7864320 | bytes 1000000 | tf_op jit(solution)/shard_map/frontier_b/pallas_call | solution.py:368
  32.5 1.3 %collective-permute-done.3.refs_10_ = f32[11,64,128]{2,1,0:T(8,128)S(1)} collective-permute-done((f32[11,64,128]{2,1,0:T(8,128)S(1)}, f32[11,64,128]{2,1,0:T(8,128)S(1)}, u32[]{:S(2)}, u32[]{:S(2)}) %collective-permute-start.3) | collective-permute-done | bytes 360480 | tf_op jit(solution)/shard_map/ppermute | solution.py:354
  33.8 2.2 %frontier_a.1 = (f32[24,2,80,128]{3,2,1,0:T(8,128)S(1)}, f32[24,2,80,128]{3,2,1,0:T(8,128)S(1)}, f32[24,2,64,128]{3,2,1,0:T(8,128)S(1)}, f32[24,2,80,128]{3,2,1,...) custom-call(f32[24,2,80,128]{3,2,1,0:T(8,128)S(1)} %get-tuple-elemen, ...), custom_call_target="tpu_custom_call", output_to_operand_aliasing={{0}: (0, {}), {1}: (1, {}), {2}: (2, {}), {3}: (3, {}), {4}... | custom-call | flops 7864320 | bytes 1000000 | tf_op jit(solution)/shard_map/frontier_a/pallas_call | solution.py:368
  36.0 5.9 %all-to-all-start = ((f32[4,96,128]{2,1,0:T(8,128)}), f32[4,96,128]{2,1,0:T(8,128)S(1)}, u32[]{:S(2)}, u32[]{:S(2)}) async-start(f32[4,96,128]{2,1,0:T(8,128)} %get-tuple-element.82), calls=%async_computation | async-start | bytes 393216 | tf_op jit(solution)/shard_map/all_to_all | solution.py:379
  41.9 1.1 %field_rows.1 = (f32[1024,128]{1,0:T(8,128)}, f32[16,128]{1,0:T(8,128)}) custom-call(f32[24,2,80,128]{3,2,1,0:T(8,128)S(1)} %get-tuple-element.78.final), custom_call_target="tpu_custom_call" | custom-call | flops 1048576 | bytes 1000000 | tf_op jit(solution)/shard_map/field_rows/pallas_call | solution.py:380
  43.0 5.7 %all-to-all-done = f32[4,96,128]{2,1,0:T(8,128)S(1)} async-done(((f32[4,96,128]{2,1,0:T(8,128)}), f32[4,96,128]{2,1,0:T(8,128)S(1)}, u32[]{:S(2)}, u32[]{:S(2)}) %all-to-all-start) | async-done | bytes 196640 | tf_op jit(solution)/shard_map/all_to_all | solution.py:379
  48.6 0.6 %multiply_reduce_fusion = f32[4]{0:T(128)} fusion(f32[4,96,128]{2,1,0:T(8,128)S(1)} %all-to-all-done, f32[96,128]{1,0:T(8,128)S(1)} %bitcast.7), kind=kLoop, calls=%fused_computation | loop fusion | flops 98300 | bytes 245776 | tf_op jit(solution)/shard_map/reduce_sum | solution.py:389
Async XLA Ops:
  3.1 11.8 %collective-permute-start = (f32[2,64,128]{2,1,0:T(8,128)S(1)}, f32[2,64,128]{2,1,0:T(8,128)S(1)}, u32[]{:S(2)}, u32[]{:S(2)}) collective-permute-start(f32[2,64,128]{2,1,0:T(8,128)S(1)} %get-tuple-element.43), channel_id=1, source_target_pairs={{1,2},{2,1},{3,4},{4,3},{5,6},{6,5},{9,10},{10,9},{11,12},{12,11},... | collective-permute-start | bytes 196616 | tf_op jit(solution)/shard_map/ppermute | solution.py:341
  3.8 11.3 %collective-permute-start.1 = (f32[2,64,128]{2,1,0:T(8,128)S(1)}, f32[2,64,128]{2,1,0:T(8,128)S(1)}, u32[]{:S(2)}, u32[]{:S(2)}) collective-permute-start(f32[2,64,128]{2,1,0:T(8,128)S(1)} %get-tuple-element.44), channel_id=1, source_target_pairs={{0,1},{1,0},{2,3},{3,2},{4,5},{5,4},{6,7},{7,6},{8,9},{9,8},{10,11... | collective-permute-start | bytes 196616 | tf_op jit(solution)/shard_map/ppermute | solution.py:342
  16.3 14.7 %collective-permute-start.2 = (f32[11,64,128]{2,1,0:T(8,128)S(1)}, f32[11,64,128]{2,1,0:T(8,128)S(1)}, u32[]{:S(2)}, u32[]{:S(2)}) collective-permute-start(f32[11,64,128]{2,1,0:T(8,128)S(1)} %get-tuple-element.66), channel_id=1, source_target_pairs={{8,16},{16,8},{24,32},{32,24},{40,48},{48,40},{56,64},{64,56},{72,... | collective-permute-start | bytes 1081352 | tf_op jit(solution)/shard_map/ppermute | solution.py:353
  21.5 12.3 %collective-permute-start.3 = (f32[11,64,128]{2,1,0:T(8,128)S(1)}, f32[11,64,128]{2,1,0:T(8,128)S(1)}, u32[]{:S(2)}, u32[]{:S(2)}) collective-permute-start(f32[11,64,128]{2,1,0:T(8,128)S(1)} %get-tuple-element.77), channel_id=1, source_target_pairs={{0,8},{8,0},{16,24},{24,16},{32,40},{40,32},{48,56},{56,48},{64,72... | collective-permute-start | bytes 1081352 | tf_op jit(solution)/shard_map/ppermute | solution.py:354
  36.0 12.6 %all-to-all-start = ((f32[4,96,128]{2,1,0:T(8,128)}), f32[4,96,128]{2,1,0:T(8,128)S(1)}, u32[]{:S(2)}, u32[]{:S(2)}) async-start(f32[4,96,128]{2,1,0:T(8,128)} %get-tuple-element.82), calls=%async_computation | async-start | bytes 393216 | tf_op jit(solution)/shard_map/all_to_all | solution.py:379

commit v5 on v4

--- a/solution.py
+++ b/solution.py
@@ -16,7 +16,7 @@
 ROWS = TX + 2 * HALO
 TOP = 8
 DEEP = NZ + 16
-CHUNK = 16
+CHUNK = 32
 STRIP = 11
 ITEMS = (("p0", 1), ("p0", 2), ("old", 1), ("p1", 2), ("p1", 3), ("p2", 3), ("wc", 1), ("wc", 2), ("p2", 4), ("wc", 3))
 VMEM = pl.BlockSpec(memory_space=pltpu.VMEM)

time: 49.6 us -> 49.6 us (level)
  no operation moved by 1% of the time
where the time goes in v5:
time: 49.6 us; the launch traced here: 49.3 us
  starting transfers between devices  24.1 us (49%)
  waiting for transfers between devices  12.6 us (25%)
  Pallas kernels  10.5 us (21%)
  between operations  1.35 us (3%)
  other arithmetic  0.63 us (1%)
    ppermute x1, starting transfers between devices, on_device(): near = lax.ppermute(near, 'gy', swap_pairs(count_y, 0))  10.5 us
    all_to_all x1, starting transfers between devices, on_device(): others = lax.all_to_all(held[10], 'sensor', 0, 0)  5.89 us
    all_to_all x1, waiting for transfers between devices, on_device(): others = lax.all_to_all(held[10], 'sensor', 0, 0)  5.66 us
    ppermute x1, waiting for transfers between devices, on_device(): strip_b = lax.ppermute(strip_b, 'gx', swap_pairs(count_x, 1))  5.43 us
    ppermute x1, starting transfers between devices, on_device(): strip_b = lax.ppermute(strip_b, 'gx', swap_pairs(count_x, 1))  5.19 us
    pallas_call x2, Pallas kernels, on_device(): pl.pallas_call(functools.partial(frontier_kernel, facing), out_shape=[sha...  3.68 us
    pallas_call x1, Pallas kernels, on_device(): pl.pallas_call(pack_kernel, out_shape=[shape(2, NZ, TY)] * 2 + [state] *...  2.48 us
    pallas_call x1, Pallas kernels, on_device(): pl.pallas_call(inner_kernel, out_shape=[state] * 2 + [coefs] + [state] *...  2.11 us
  transfers between devices with their start and end apart: 5, of which 4 were waited for; matrix products, arithmetic and copies ran while one was open for 0% of the time, Pallas kernels for 9%

profile of v5, /device:TPU:6, one launch (start us, length us, event | category | flops | bytes accessed | tf_op | source)
XLA Modules:
  0.0 49.3 jit_solution(14735885901216058731)
XLA Ops:
  0.6 2.5 %pack_columns.1 = (f32[2,64,128]{2,1,0:T(8,128)S(1)}, f32[2,64,128]{2,1,0:T(8,128)S(1)}, f32[24,2,80,128]{3,2,1,0:T(8,128)S(1)}, f32[24,2,80,128]{3,2,1,0:T(8,12...) custom-call(f32[1024,128]{1,0:T(8,128)} %bitcast.8, f32[1024,128]{1,0:T(8,128)} %bitcast.9, ...), custom_call_target="tpu_custom_call" | custom-call | tf_op jit(solution)/shard_map/pack_columns/pallas_call | solution.py:329
  3.1 0.7 %collective-permute-start = (f32[2,64,128]{2,1,0:T(8,128)S(1)}, f32[2,64,128]{2,1,0:T(8,128)S(1)}, u32[]{:S(2)}, u32[]{:S(2)}) collective-permute-start(f32[2,64,128]{2,1,0:T(8,128)S(1)} %get-tuple-element.43), channel_id=1, source_target_pairs={{1,2},{2,1},{3,4},{4,3},{5,6},{6,5},{9,10},{10,9},{11,12},{12,11},... | collective-permute-start | bytes 196616 | tf_op jit(solution)/shard_map/ppermute | solution.py:341
  3.8 10.5 %collective-permute-start.1 = (f32[2,64,128]{2,1,0:T(8,128)S(1)}, f32[2,64,128]{2,1,0:T(8,128)S(1)}, u32[]{:S(2)}, u32[]{:S(2)}) collective-permute-start(f32[2,64,128]{2,1,0:T(8,128)S(1)} %get-tuple-element.44), channel_id=1, source_target_pairs={{0,1},{1,0},{2,3},{3,2},{4,5},{5,4},{6,7},{7,6},{8,9},{9,8},{10,11... | collective-permute-start | bytes 196616 | tf_op jit(solution)/shard_map/ppermute | solution.py:342
  14.9 0.0 collective-permute-done.far
  14.9 0.2 collective-permute-done.1.near
  15.1 1.2 %edge_rows.1 = (f32[11,64,128]{2,1,0:T(8,128)S(1)}, f32[11,64,128]{2,1,0:T(8,128)S(1)}, f32[24,2,80,128]{3,2,1,0:T(8,128)S(1)}, f32[24,2,80,128]{3,2,1,0:T(8,128...) custom-call(f32[2,64,128]{2,1,0:T(8,128)S(1)} %collective-permute-do, ...), custom_call_target="tpu_custom_call", output_to_operand_aliasing={{2}: (2, {}), {3}: (3, {}), {4}: (4, {})} | custom-call | flops 3145728 | bytes 1000000 | tf_op jit(solution)/shard_map/edge_rows/pallas_call | solution.py:343
  16.3 5.2 %collective-permute-start.2 = (f32[11,64,128]{2,1,0:T(8,128)S(1)}, f32[11,64,128]{2,1,0:T(8,128)S(1)}, u32[]{:S(2)}, u32[]{:S(2)}) collective-permute-start(f32[11,64,128]{2,1,0:T(8,128)S(1)} %get-tuple-element.66), channel_id=1, source_target_pairs={{8,16},{16,8},{24,32},{32,24},{40,48},{48,40},{56,64},{64,56},{72,... | collective-permute-start | bytes 1081352 | tf_op jit(solution)/shard_map/ppermute | solution.py:353
  21.5 1.9 %collective-permute-start.3 = (f32[11,64,128]{2,1,0:T(8,128)S(1)}, f32[11,64,128]{2,1,0:T(8,128)S(1)}, u32[]{:S(2)}, u32[]{:S(2)}) collective-permute-start(f32[11,64,128]{2,1,0:T(8,128)S(1)} %get-tuple-element.77), channel_id=1, source_target_pairs={{0,8},{8,0},{16,24},{24,16},{32,40},{40,32},{48,56},{56,48},{64,72... | collective-permute-start | bytes 1081352 | tf_op jit(solution)/shard_map/ppermute | solution.py:354
  23.5 2.1 %inner_rows.1 = (f32[24,2,80,128]{3,2,1,0:T(8,128)S(1)}, f32[24,2,80,128]{3,2,1,0:T(8,128)S(1)}, f32[24,2,64,128]{3,2,1,0:T(8,128)S(1)}, f32[24,2,80,128]{3,2,1,...) custom-call(f32[24,2,80,128]{3,2,1,0:T(8,128)S(1)} %get-tuple-elemen, ...), custom_call_target="tpu_custom_call", output_to_operand_aliasing={{0}: (0, {}), {1}: (1, {}), {2}: (2, {}), {3}: (3, {}), {4}... | custom-call | flops 13107200 | bytes 1000000 | tf_op jit(solution)/shard_map/inner_rows/pallas_call | solution.py:355
  25.6 5.4 %collective-permute-done.2.refs_10_ = f32[11,64,128]{2,1,0:T(8,128)S(1)} collective-permute-done((f32[11,64,128]{2,1,0:T(8,128)S(1)}, f32[11,64,128]{2,1,0:T(8,128)S(1)}, u32[]{:S(2)}, u32[]{:S(2)}) %collective-permute-start.2) | collective-permute-done | bytes 360480 | tf_op jit(solution)/shard_map/ppermute | solution.py:353
  31.0 1.5 %frontier_b.1 = (f32[24,2,80,128]{3,2,1,0:T(8,128)S(1)}, f32[24,2,80,128]{3,2,1,0:T(8,128)S(1)}, f32[24,2,64,128]{3,2,1,0:T(8,128)S(1)}, f32[24,2,80,128]{3,2,1,...) custom-call(f32[24,2,80,128]{3,2,1,0:T(8,128)S(1)} %get-tuple-elemen, ...), custom_call_target="tpu_custom_call", output_to_operand_aliasing={{0}: (0, {}), {1}: (1, {}), {2}: (2, {}), {3}: (3, {}), {4}... | custom-call | flops 7864320 | bytes 1000000 | tf_op jit(solution)/shard_map/frontier_b/pallas_call | solution.py:368
  32.5 1.3 %collective-permute-done.3.refs_10_ = f32[11,64,128]{2,1,0:T(8,128)S(1)} collective-permute-done((f32[11,64,128]{2,1,0:T(8,128)S(1)}, f32[11,64,128]{2,1,0:T(8,128)S(1)}, u32[]{:S(2)}, u32[]{:S(2)}) %collective-permute-start.3) | collective-permute-done | bytes 360480 | tf_op jit(solution)/shard_map/ppermute | solution.py:354
  33.8 2.2 %frontier_a.1 = (f32[24,2,80,128]{3,2,1,0:T(8,128)S(1)}, f32[24,2,80,128]{3,2,1,0:T(8,128)S(1)}, f32[24,2,64,128]{3,2,1,0:T(8,128)S(1)}, f32[24,2,80,128]{3,2,1,...) custom-call(f32[24,2,80,128]{3,2,1,0:T(8,128)S(1)} %get-tuple-elemen, ...), custom_call_target="tpu_custom_call", output_to_operand_aliasing={{0}: (0, {}), {1}: (1, {}), {2}: (2, {}), {3}: (3, {}), {4}... | custom-call | flops 7864320 | bytes 1000000 | tf_op jit(solution)/shard_map/frontier_a/pallas_call | solution.py:368
  36.0 5.9 %all-to-all-start = ((f32[4,96,128]{2,1,0:T(8,128)}), f32[4,96,128]{2,1,0:T(8,128)S(1)}, u32[]{:S(2)}, u32[]{:S(2)}) async-start(f32[4,96,128]{2,1,0:T(8,128)} %get-tuple-element.82), calls=%async_computation | async-start | bytes 393216 | tf_op jit(solution)/shard_map/all_to_all | solution.py:379
  41.9 1.1 %field_rows.1 = (f32[1024,128]{1,0:T(8,128)}, f32[16,128]{1,0:T(8,128)}) custom-call(f32[24,2,80,128]{3,2,1,0:T(8,128)S(1)} %get-tuple-element.78.final), custom_call_target="tpu_custom_call" | custom-call | flops 1048576 | bytes 1000000 | tf_op jit(solution)/shard_map/field_rows/pallas_call | solution.py:380
  43.0 5.7 %all-to-all-done = f32[4,96,128]{2,1,0:T(8,128)S(1)} async-done(((f32[4,96,128]{2,1,0:T(8,128)}), f32[4,96,128]{2,1,0:T(8,128)S(1)}, u32[]{:S(2)}, u32[]{:S(2)}) %all-to-all-start) | async-done | bytes 196640 | tf_op jit(solution)/shard_map/all_to_all | solution.py:379
  48.6 0.6 %multiply_reduce_fusion = f32[4]{0:T(128)} fusion(f32[4,96,128]{2,1,0:T(8,128)S(1)} %all-to-all-done, f32[96,128]{1,0:T(8,128)S(1)} %bitcast.7), kind=kLoop, calls=%fused_computation | loop fusion | flops 98300 | bytes 245776 | tf_op jit(solution)/shard_map/reduce_sum | solution.py:389
Async XLA Ops:
  3.1 11.8 %collective-permute-start = (f32[2,64,128]{2,1,0:T(8,128)S(1)}, f32[2,64,128]{2,1,0:T(8,128)S(1)}, u32[]{:S(2)}, u32[]{:S(2)}) collective-permute-start(f32[2,64,128]{2,1,0:T(8,128)S(1)} %get-tuple-element.43), channel_id=1, source_target_pairs={{1,2},{2,1},{3,4},{4,3},{5,6},{6,5},{9,10},{10,9},{11,12},{12,11},... | collective-permute-start | bytes 196616 | tf_op jit(solution)/shard_map/ppermute | solution.py:341
  3.8 11.3 %collective-permute-start.1 = (f32[2,64,128]{2,1,0:T(8,128)S(1)}, f32[2,64,128]{2,1,0:T(8,128)S(1)}, u32[]{:S(2)}, u32[]{:S(2)}) collective-permute-start(f32[2,64,128]{2,1,0:T(8,128)S(1)} %get-tuple-element.44), channel_id=1, source_target_pairs={{0,1},{1,0},{2,3},{3,2},{4,5},{5,4},{6,7},{7,6},{8,9},{9,8},{10,11... | collective-permute-start | bytes 196616 | tf_op jit(solution)/shard_map/ppermute | solution.py:342
  16.3 14.7 %collective-permute-start.2 = (f32[11,64,128]{2,1,0:T(8,128)S(1)}, f32[11,64,128]{2,1,0:T(8,128)S(1)}, u32[]{:S(2)}, u32[]{:S(2)}) collective-permute-start(f32[11,64,128]{2,1,0:T(8,128)S(1)} %get-tuple-element.66), channel_id=1, source_target_pairs={{8,16},{16,8},{24,32},{32,24},{40,48},{48,40},{56,64},{64,56},{72,... | collective-permute-start | bytes 1081352 | tf_op jit(solution)/shard_map/ppermute | solution.py:353
  21.5 12.3 %collective-permute-start.3 = (f32[11,64,128]{2,1,0:T(8,128)S(1)}, f32[11,64,128]{2,1,0:T(8,128)S(1)}, u32[]{:S(2)}, u32[]{:S(2)}) collective-permute-start(f32[11,64,128]{2,1,0:T(8,128)S(1)} %get-tuple-element.77), channel_id=1, source_target_pairs={{0,8},{8,0},{16,24},{24,16},{32,40},{40,32},{48,56},{56,48},{64,72... | collective-permute-start | bytes 1081352 | tf_op jit(solution)/shard_map/ppermute | solution.py:354
  36.0 12.6 %all-to-all-start = ((f32[4,96,128]{2,1,0:T(8,128)}), f32[4,96,128]{2,1,0:T(8,128)S(1)}, u32[]{:S(2)}, u32[]{:S(2)}) async-start(f32[4,96,128]{2,1,0:T(8,128)} %get-tuple-element.82), calls=%async_computation | async-start | bytes 393216 | tf_op jit(solution)/shard_map/all_to_all | solution.py:379
